TPU v7x, 512 devices: a whole 4x4x16 slice. The times are simulated.
512 devices in a mesh: dom: 128 (over x, z, core), sub: 4 (over y).
Axes of the slice: x: 4, y: 4, z: 16, core: 2. Of those that a mesh axis runs over, the one named last changes fastest.
Arguments:
- feats: bfloat16 [256, 49152], P('sub', 'dom'), may hold values from -6 to 6
- weight: bfloat16 [27, 256, 256], P(None, 'sub'), may hold values from -0.078125 to 0.078125
- grad_out: bfloat16 [256, 49152], P('sub', 'dom'), may hold values from -6 to 6
- neighbors: int32 [27, 49152], P(None, 'dom'), may hold values from -1 to 639, as said below
- send_rows: int32 [128, 256], P('dom'), may hold values from 0 to 383
- send_counts: int32 [128, 8], replicated, may hold values from 0 to 32, as said below
Outputs:
- out_feats: bfloat16 [256, 49152], P('sub', 'dom')
- grad_feats: float32 [256, 49152], P('sub', 'dom')
- grad_weight: float32 [27, 256, 256], P(None, 'sub')
Inputs may be any that keep to these rules, and one draw needn't show every extreme that they name: neighbors[k, v] names the row of the table of v's partition that feeds v at offset k: values below 384 are the partition's own voxels, a value 384 + n * 32 + j names a received row with j below the count that arrives from direction n; -1 marks an absent neighbour; the middle offset names the voxel itself. send_counts[s, n] rows, the first ones of slots n * 32 onward of s's list, go from partition s to its neighbour in direction n; the count is 0 where that neighbour lies outside the grid, and positive otherwise.
All inputs are finite; a program needn't handle non-finite values.
Results may differ from a plain program's by a relative error of at most 0.001.
Values may be sent and summed in bfloat16 or wider, within the bound.
A program may use at most 64 MiB of HBM per device.

v0:
```python
import math

import jax
import jax.numpy as jnp
from jax import lax
from jax.sharding import PartitionSpec as P

C = 256
KVOL = 27
CAP = 32


DIRECTIONS = ((-1, -1), (-1, 0), (-1, 1), (0, -1), (0, 1), (1, -1), (1, 0), (1, 1))


def from_behind(block, axis, distance):
    devices = range(lax.axis_size(axis))
    route = [(i - distance, i) for i in devices if i - distance in devices]
    return lax.ppermute(block, axis, route)


def move_tiles(tiles, backward, grid_y):
    sign = -1 if backward else 1
    current = list(tiles)
    for direction, (step_x, step_y) in enumerate(DIRECTIONS):
        hop = sign * (step_x * grid_y + step_y)
        if backward:
            current[direction] = from_behind(current[direction], "dom", hop)
        else:
            current[direction] = from_behind(current[direction], "dom", hop)
    return current


def spread_table(w_part, cotangent, nbr_flat, valid_flat, total_cols):
    spread = lax.dot_general(
        w_part, cotangent, (((1,), (0,)), ((), ())), preferred_element_type=jnp.float32
    )
    spread = jnp.transpose(spread, (1, 0, 2))
    rows_here = spread.shape[0]
    spread = spread.reshape(rows_here, -1)
    spread = jnp.where(valid_flat[None, :], spread, 0.0)
    return jnp.zeros((rows_here, total_cols), jnp.float32).at[:, nbr_flat].add(spread)


def body(feats, weight, grad_out, neighbors, send_rows, send_counts):
    shard_ch, local_vox = feats.shape
    n_dom = lax.axis_size("dom")
    grid_y = min(8, n_dom // 2)
    my_index = lax.axis_index("dom")
    halo_cols = 8 * CAP
    total_cols = local_vox + halo_cols
    counts_out = lax.dynamic_slice_in_dim(send_counts, my_index, 1, 0)[0]
    slot_pos = jnp.arange(halo_cols, dtype=jnp.int32) % CAP
    send_mask = slot_pos < jnp.repeat(counts_out, CAP, total_repeat_length=halo_cols)
    out_rows = send_rows[0]
    outgoing = jnp.where(send_mask[None, :], feats[:, out_rows], jnp.zeros((), feats.dtype))
    tiles_out = [outgoing[:, n * CAP : (n + 1) * CAP] for n in range(8)]
    received = jnp.concatenate(move_tiles(tiles_out, False, grid_y), axis=1)
    table = jnp.concatenate([feats, received], axis=1)
    nbr_index = jnp.maximum(neighbors, 0)
    nbr_valid = neighbors >= 0
    nbr_flat = nbr_index.reshape(-1)
    valid_flat = nbr_valid.reshape(-1)
    segment = lax.all_gather(table, "sub", axis=0, tiled=True)
    anchor = jnp.int32(0)
    out_acc = jnp.zeros((shard_ch, local_vox), jnp.float32)
    wgrad_acc = jnp.zeros((KVOL, shard_ch, C), jnp.float32)
    seg_rows = segment.shape[0]
    gathered = jnp.where(nbr_valid[None, :, :], segment[:, nbr_index], jnp.zeros((), segment.dtype))
    w_cols = lax.dynamic_slice_in_dim(weight, anchor, seg_rows, 2)
    out_acc = out_acc + lax.dot_general(
        w_cols, gathered, (((0, 2), (1, 0)), ((), ())), preferred_element_type=jnp.float32
    )
    fresh = lax.dot_general(
        grad_out, gathered, (((1,), (2,)), ((), ())), preferred_element_type=jnp.float32
    )
    fresh_terms = jnp.transpose(fresh, (2, 0, 1))
    zero_idx = jnp.zeros((), jnp.int32)
    anchor_idx = jnp.asarray(anchor, jnp.int32)
    former = lax.dynamic_slice(
        wgrad_acc, (zero_idx, zero_idx, anchor_idx), (KVOL, shard_ch, seg_rows)
    )
    wgrad_acc = lax.dynamic_update_slice(
        wgrad_acc, former + fresh_terms, (zero_idx, zero_idx, anchor_idx)
    )
    out_acc, wgrad_local = (out_acc, wgrad_acc)
    out_feats = out_acc.astype(jnp.bfloat16)
    grad_weight = lax.psum(wgrad_local, "dom") * (1.0 / math.sqrt(local_vox * n_dom))
    table_grad = lax.psum_scatter(
        spread_table(weight, grad_out, nbr_flat, valid_flat, total_cols),
        "sub",
        scatter_dimension=0,
        tiled=True,
    )
    halo_grad = table_grad[:, local_vox:]
    tiles_back = [halo_grad[:, n * CAP : (n + 1) * CAP] for n in range(8)]
    returned = jnp.concatenate(move_tiles(tiles_back, True, grid_y), axis=1)
    grad_feats = (
        table_grad[:, :local_vox].at[:, out_rows].add(jnp.where(send_mask[None, :], returned, 0.0))
    )
    return (out_feats, grad_feats, grad_weight)


def solution(mesh):
    in_specs = (
        P("sub", "dom"),
        P(None, "sub", None),
        P("sub", "dom"),
        P(None, "dom"),
        P("dom", None),
        P(),
    )
    out_specs = (P("sub", "dom"), P("sub", "dom"), P(None, "sub", None))
    return jax.shard_map(body, mesh=mesh, in_specs=in_specs, out_specs=out_specs, check_vma=False)
```

profile of v0, /device:TPU:1, one launch (start us, length us, event | category | flops | bytes accessed | tf_op | source)
XLA Modules:
  0.0 593.7 jit_solution(13790902209037114251)
XLA Ops:
  8.1 0.9 broadcast_compare_fusion
  8.9 0.8 fusion.32
  9.8 6.3 %convolution_bitcast_fusion = f32[256,27,384]{2,0,1:T(8,128)} fusion(bf16[27,64,256]{2,1,0:T(8,128)(2,1)S(1)} %copy-done, bf16[64,384]{1,0:T(8,128)(2,1)} %param.10), kind=kOutput, calls=%fused_computation.12 | convolution fusion | flops 339738624 | bytes 11550720 | tf_op jit(solution)/shard_map/dot_general | solution.py:35
  16.1 11.6 %copy.29 = f32[256,27,384]{0,2,1:T(8,128)} copy(f32[256,27,384]{2,0,1:T(8,128)} %convolution_bitcast_fusion) | data formatting | bytes 21233664 | tf_op jit(solution)/shard_map/transpose | solution.py:38
  27.7 0.1 fusion.28
  27.8 12.3 %bitcast_select_fusion = f32[256,10368]{0,1:T(8,128)} fusion(f32[256,27,384]{0,2,1:T(8,128)} %copy.29, pred[10368]{0:T(1024)(128)(4,1)S(1)} %broadcast_in_dim.74), kind=kLoop, calls=%fused_computation.6 | loop fusion | flops 2654208 | bytes 21244032 | tf_op jit(solution)/shard_map/jit(_where)/select_n | solution.py:41
  40.1 56.4 %scatter_custom_fusion = f32[256,640]{0,1:T(8,128)S(1)} fusion(s32[10368]{0:T(1024)S(1)} %fusion.28, f32[256,10368]{0,1:T(8,128)} %bitcast_select_fusion, f32[]{:T(128)} %constant.125.clone.1), kind=kCustom, calls=%fused_computation.4 | custom fusion | flops 2654208 | bytes 11272196 | tf_op jit(solution)/shard_map/scatter-add | solution.py:42
  96.5 1.1 copy.31
  97.7 0.1 constant_dynamic-slice_fusion
  97.8 0.6 fusion.35
  98.4 0.1 add_add_fusion.1
  98.5 4.5 compare_select_fusion.3
  103.0 0.7 fusion.29
  103.7 0.1 copy.18
  103.9 0.9 gather_fusion
  104.7 0.1 select_bitcast_fusion
  104.8 1.3 collective-permute-start
  106.1 1.3 collective-permute-start.1
  107.4 1.3 collective-permute-start.2
  108.7 8.8 %collective-permute-start.3 = (bf16[64,32]{0,1:T(8,128)(2,1)S(1)}, bf16[64,32]{0,1:T(8,128)(2,1)S(1)}, u32[]{:S(2)}, u32[]{:S(2)}) collective-permute-start(bf16[64,32]{0,1:T(8,128)(2,1)S(1)} %get-tuple-element.36), channel_id=1, source_target_pairs={{4,0},{8,4},{12,8},{16,12},{20,16},{24,20},{28,24},{32,28},{36,32}... | collective-permute-start | bytes 12296 | tf_op jit(solution)/shard_map/ppermute | solution.py:19
  117.5 1.9 collective-permute-start.4
  119.5 9.4 %collective-permute-start.5 = (bf16[64,32]{0,1:T(8,128)(2,1)S(1)}, bf16[64,32]{0,1:T(8,128)(2,1)S(1)}, u32[]{:S(2)}, u32[]{:S(2)}) collective-permute-start(bf16[64,32]{0,1:T(8,128)(2,1)S(1)} %get-tuple-element.34), channel_id=1, source_target_pairs={{0,28},{4,32},{8,36},{12,40},{16,44},{20,48},{24,52},{28,56},{32,6... | collective-permute-start | bytes 12296 | tf_op jit(solution)/shard_map/ppermute | solution.py:19
  128.9 7.7 %collective-permute-start.6 = (bf16[64,32]{0,1:T(8,128)(2,1)S(1)}, bf16[64,32]{0,1:T(8,128)(2,1)S(1)}, u32[]{:S(2)}, u32[]{:S(2)}) collective-permute-start(bf16[64,32]{0,1:T(8,128)(2,1)S(1)} %get-tuple-element.33), channel_id=1, source_target_pairs={{0,32},{4,36},{8,40},{12,44},{16,48},{20,52},{24,56},{28,60},{32,6... | collective-permute-start | bytes 12296 | tf_op jit(solution)/shard_map/ppermute | solution.py:19
  136.6 7.4 %collective-permute-start.7 = (bf16[64,32]{0,1:T(8,128)(2,1)S(1)}, bf16[64,32]{0,1:T(8,128)(2,1)S(1)}, u32[]{:S(2)}, u32[]{:S(2)}) collective-permute-start(bf16[64,32]{0,1:T(8,128)(2,1)S(1)} %get-tuple-element.32), channel_id=1, source_target_pairs={{0,36},{4,40},{8,44},{12,48},{16,52},{20,56},{24,60},{28,64},{32,6... | collective-permute-start | bytes 12296 | tf_op jit(solution)/shard_map/ppermute | solution.py:19
  144.1 0.1 copy.19
  144.2 0.1 copy.20
  144.3 0.1 copy.21
  144.4 0.1 copy.22
  144.5 0.1 copy.23
  144.6 0.1 copy.24
  144.7 0.1 copy.25
  144.8 0.1 copy.26
  144.9 0.1 concatenate.10
  145.1 9.5 %all_gather.3 = bf16[256,640]{1,0:T(8,128)(2,1)S(1)} all-gather(bf16[64,640]{1,0:T(8,128)(2,1)S(1)} %concatenate.10), channel_id=1, replica_groups=mesh['dom'=128,'sub'=4] {'sub'}, dimensions={0}, use_global_device_ids=true | all-gather | bytes 409600 | tf_op jit(solution)/shard_map/all_gather | solution.py:64
  154.6 0.2 copy.27
  154.8 29.8 %gather_fusion.1 = bf16[10368,256]{1,0:T(8,128)(2,1)} fusion(bf16[256,640]{0,1:T(8,128)(2,1)S(1)} %copy.27, s32[11264]{0:T(1024)S(1)} %pad_clamp_fusion), kind=kCustom, calls=%fused_computation.1 | custom fusion | bytes 10658304 | tf_op jit(solution)/shard_map/gather | solution.py:69
  184.6 8.0 %copy.28 = bf16[27,384,256]{1,2,0:T(8,128)(2,1)} copy(bf16[27,384,256]{2,1,0:T(8,128)(2,1)} %bitcast.67) | data formatting | bytes 10616832 | tf_op jit(solution)/shard_map/gather | solution.py:69
  192.6 5.5 fusion.8
  198.1 4.1 fusion.17
  202.2 1.2 fusion.33
  203.4 0.1 copy.34
  203.5 11.9 %collective-permute-start.8 = (f32[64,32]{0,1:T(8,128)S(1)}, f32[64,32]{0,1:T(8,128)S(1)}, u32[]{:S(2)}, u32[]{:S(2)}) collective-permute-start(f32[64,32]{0,1:T(8,128)S(1)} %copy.34), channel_id=1, source_target_pairs={{0,36},{4,40},{8,44},{12,48},{16,52},{20,56},{24,60},{28,64},{32,6... | collective-permute-start | bytes 24584 | tf_op jit(solution)/shard_map/ppermute | solution.py:19
  215.4 333.5 %all-reduce.2.cloned.1.call-done = f32[27,64,256]{2,1,0:T(8,128)} async-done(((f32[27,64,256]{2,1,0:T(8,128)}), f32[27,64,256]{2,1,0:T(8,128)}) %all-reduce.2.cloned.1.call-update) | async-done | bytes 1769488 | tf_op jit(solution)/shard_map/psum | solution.py:88
  548.8 2.9 broadcast_multiply_fusion
  551.8 3.2 collective-permute-start.9
  555.1 0.1 copy.36
  555.1 9.3 %collective-permute-start.10 = (f32[64,32]{0,1:T(8,128)S(1)}, f32[64,32]{0,1:T(8,128)S(1)}, u32[]{:S(2)}, u32[]{:S(2)}) collective-permute-start(f32[64,32]{0,1:T(8,128)S(1)} %copy.36), channel_id=1, source_target_pairs={{0,28},{4,32},{8,36},{12,40},{16,44},{20,48},{24,52},{28,56},{32,6... | collective-permute-start | bytes 24584 | tf_op jit(solution)/shard_map/ppermute | solution.py:19
  564.4 0.1 copy.37
  564.5 1.9 collective-permute-start.11
  566.4 0.1 copy.38
  566.5 2.4 collective-permute-start.12
  568.9 0.1 copy.39
  568.9 0.1 copy.40
  569.0 0.1 copy.41
  569.1 0.9 slice.123
  570.0 0.1 copy.33
  570.1 1.3 collective-permute-start.13
  571.5 1.3 collective-permute-start.14
  572.8 1.3 collective-permute-start.15
  574.1 5.1 collective-permute-done.13
  579.2 1.3 collective-permute-done.14
  580.6 2.8 collective-permute-done.15
  583.4 2.1 scatter_custom_fusion.1
  585.5 0.8 copy.30
  (48 shorter events, 0.4 us)
Async XLA Ops:
  8.0 1.8 copy-start
  8.0 194.2 %reduce-scatter.4.cloned.1.call-start = ((), (), s32[]{:S(2)}) async-start(), calls=%async_computation.2 | async-start | bytes 819200
  40.1 57.6 %copy-start.3 = (s32[128,8]{0,1:T(8,128)S(1)}, s32[128,8]{0,1:T(8,128)}, u32[]{:S(2)}) copy-start(s32[128,8]{0,1:T(8,128)} %param.13) | copy-start | bytes 12292
  40.1 58.3 %copy-start.5 = (s32[1,256]{1,0:T(1,128)S(1)}, s32[1,256]{1,0:T(1,128)}, u32[]{:S(2)}) copy-start(s32[1,256]{1,0:T(1,128)} %param.12) | copy-start | bytes 3076
  40.1 58.3 %copy-start.4 = (s32[2,128]{1,0:T(2,128)S(1)}, s32[2,128]{1,0:T(2,128)}, u32[]{:S(2)}) copy-start(s32[2,128]{1,0:T(2,128)} %constant.116.clone.1) | copy-start | bytes 3076
  40.1 63.6 %copy-start.1 = (bf16[64,384]{1,0:T(8,128)(2,1)S(1)}, bf16[64,384]{1,0:T(8,128)(2,1)}, u32[]{:S(2)}) copy-start(bf16[64,384]{1,0:T(8,128)(2,1)} %param.8) | copy-start | bytes 147460
  97.6 451.2 %all-reduce.2.cloned.1.call-start = ((), (), s32[]{:S(2)}) async-start(), calls=%async_computation.1 | async-start | bytes 3538944 | tf_op jit(solution)/shard_map/psum | solution.py:88
  104.8 14.6 %collective-permute-start = (bf16[64,32]{0,1:T(8,128)(2,1)S(1)}, bf16[64,32]{0,1:T(8,128)(2,1)S(1)}, u32[]{:S(2)}, u32[]{:S(2)}) collective-permute-start(bf16[64,32]{0,1:T(8,128)(2,1)S(1)} %get-tuple-element.39), channel_id=1, source_target_pairs={{36,0},{40,4},{44,8},{48,12},{52,16},{56,20},{60,24},{64,28},{68,3... | collective-permute-start | bytes 12296 | tf_op jit(solution)/shard_map/ppermute | solution.py:19
  106.1 22.8 %collective-permute-start.1 = (bf16[64,32]{0,1:T(8,128)(2,1)S(1)}, bf16[64,32]{0,1:T(8,128)(2,1)S(1)}, u32[]{:S(2)}, u32[]{:S(2)}) collective-permute-start(bf16[64,32]{0,1:T(8,128)(2,1)S(1)} %get-tuple-element.38), channel_id=1, source_target_pairs={{32,0},{36,4},{40,8},{44,12},{48,16},{52,20},{56,24},{60,28},{64,3... | collective-permute-start | bytes 12296 | tf_op jit(solution)/shard_map/ppermute | solution.py:19
  107.4 29.2 %collective-permute-start.2 = (bf16[64,32]{0,1:T(8,128)(2,1)S(1)}, bf16[64,32]{0,1:T(8,128)(2,1)S(1)}, u32[]{:S(2)}, u32[]{:S(2)}) collective-permute-start(bf16[64,32]{0,1:T(8,128)(2,1)S(1)} %get-tuple-element.37), channel_id=1, source_target_pairs={{28,0},{32,4},{36,8},{40,12},{44,16},{48,20},{52,24},{56,28},{60,3... | collective-permute-start | bytes 12296 | tf_op jit(solution)/shard_map/ppermute | solution.py:19
  108.7 35.6 %collective-permute-start.3 = (bf16[64,32]{0,1:T(8,128)(2,1)S(1)}, bf16[64,32]{0,1:T(8,128)(2,1)S(1)}, u32[]{:S(2)}, u32[]{:S(2)}) collective-permute-start(bf16[64,32]{0,1:T(8,128)(2,1)S(1)} %get-tuple-element.36), channel_id=1, source_target_pairs={{4,0},{8,4},{12,8},{16,12},{20,16},{24,20},{28,24},{32,28},{36,32}... | collective-permute-start | bytes 12296 | tf_op jit(solution)/shard_map/ppermute | solution.py:19
  117.5 27.0 %collective-permute-start.4 = (bf16[64,32]{0,1:T(8,128)(2,1)S(1)}, bf16[64,32]{0,1:T(8,128)(2,1)S(1)}, u32[]{:S(2)}, u32[]{:S(2)}) collective-permute-start(bf16[64,32]{0,1:T(8,128)(2,1)S(1)} %get-tuple-element.35), channel_id=1, source_target_pairs={{0,4},{4,8},{8,12},{12,16},{16,20},{20,24},{24,28},{28,32},{32,36}... | collective-permute-start | bytes 12296 | tf_op jit(solution)/shard_map/ppermute | solution.py:19
  119.5 25.1 %collective-permute-start.5 = (bf16[64,32]{0,1:T(8,128)(2,1)S(1)}, bf16[64,32]{0,1:T(8,128)(2,1)S(1)}, u32[]{:S(2)}, u32[]{:S(2)}) collective-permute-start(bf16[64,32]{0,1:T(8,128)(2,1)S(1)} %get-tuple-element.34), channel_id=1, source_target_pairs={{0,28},{4,32},{8,36},{12,40},{16,44},{20,48},{24,52},{28,56},{32,6... | collective-permute-start | bytes 12296 | tf_op jit(solution)/shard_map/ppermute | solution.py:19
  128.9 15.8 %collective-permute-start.6 = (bf16[64,32]{0,1:T(8,128)(2,1)S(1)}, bf16[64,32]{0,1:T(8,128)(2,1)S(1)}, u32[]{:S(2)}, u32[]{:S(2)}) collective-permute-start(bf16[64,32]{0,1:T(8,128)(2,1)S(1)} %get-tuple-element.33), channel_id=1, source_target_pairs={{0,32},{4,36},{8,40},{12,44},{16,48},{20,52},{24,56},{28,60},{32,6... | collective-permute-start | bytes 12296 | tf_op jit(solution)/shard_map/ppermute | solution.py:19
  136.6 8.2 %collective-permute-start.7 = (bf16[64,32]{0,1:T(8,128)(2,1)S(1)}, bf16[64,32]{0,1:T(8,128)(2,1)S(1)}, u32[]{:S(2)}, u32[]{:S(2)}) collective-permute-start(bf16[64,32]{0,1:T(8,128)(2,1)S(1)} %get-tuple-element.32), channel_id=1, source_target_pairs={{0,36},{4,40},{8,44},{12,48},{16,52},{20,56},{24,60},{28,64},{32,6... | collective-permute-start | bytes 12296 | tf_op jit(solution)/shard_map/ppermute | solution.py:19
  184.6 8.0 %copy-start.2 = (bf16[64,384]{1,0:T(8,128)(2,1)S(1)}, bf16[64,384]{1,0:T(8,128)(2,1)}, u32[]{:S(2)}) copy-start(bf16[64,384]{1,0:T(8,128)(2,1)} %param.10) | copy-start | bytes 147460
  203.5 366.7 %collective-permute-start.8 = (f32[64,32]{0,1:T(8,128)S(1)}, f32[64,32]{0,1:T(8,128)S(1)}, u32[]{:S(2)}, u32[]{:S(2)}) collective-permute-start(f32[64,32]{0,1:T(8,128)S(1)} %copy.34), channel_id=1, source_target_pairs={{0,36},{4,40},{8,44},{12,48},{16,52},{20,56},{24,60},{28,64},{32,6... | collective-permute-start | bytes 24584 | tf_op jit(solution)/shard_map/ppermute | solution.py:19
  551.8 19.6 %collective-permute-start.9 = (f32[64,32]{0,1:T(8,128)S(1)}, f32[64,32]{0,1:T(8,128)S(1)}, u32[]{:S(2)}, u32[]{:S(2)}) collective-permute-start(f32[64,32]{0,1:T(8,128)S(1)} %copy.35), channel_id=1, source_target_pairs={{0,32},{4,36},{8,40},{12,44},{16,48},{20,52},{24,56},{28,60},{32,6... | collective-permute-start | bytes 24584 | tf_op jit(solution)/shard_map/ppermute | solution.py:19
  555.1 17.7 %collective-permute-start.10 = (f32[64,32]{0,1:T(8,128)S(1)}, f32[64,32]{0,1:T(8,128)S(1)}, u32[]{:S(2)}, u32[]{:S(2)}) collective-permute-start(f32[64,32]{0,1:T(8,128)S(1)} %copy.36), channel_id=1, source_target_pairs={{0,28},{4,32},{8,36},{12,40},{16,44},{20,48},{24,52},{28,56},{32,6... | collective-permute-start | bytes 24584 | tf_op jit(solution)/shard_map/ppermute | solution.py:19
  564.5 9.6 %collective-permute-start.11 = (f32[64,32]{0,1:T(8,128)S(1)}, f32[64,32]{0,1:T(8,128)S(1)}, u32[]{:S(2)}, u32[]{:S(2)}) collective-permute-start(f32[64,32]{0,1:T(8,128)S(1)} %copy.37), channel_id=1, source_target_pairs={{0,4},{4,8},{8,12},{12,16},{16,20},{20,24},{24,28},{28,32},{32,36}... | collective-permute-start | bytes 24584 | tf_op jit(solution)/shard_map/ppermute | solution.py:19
  566.5 7.7 %collective-permute-start.12 = (f32[64,32]{0,1:T(8,128)S(1)}, f32[64,32]{0,1:T(8,128)S(1)}, u32[]{:S(2)}, u32[]{:S(2)}) collective-permute-start(f32[64,32]{0,1:T(8,128)S(1)} %copy.38), channel_id=1, source_target_pairs={{4,0},{8,4},{12,8},{16,12},{20,16},{24,20},{28,24},{32,28},{36,32}... | collective-permute-start | bytes 24584 | tf_op jit(solution)/shard_map/ppermute | solution.py:19
  570.1 9.1 %collective-permute-start.13 = (f32[64,32]{0,1:T(8,128)S(1)}, f32[64,32]{0,1:T(8,128)S(1)}, u32[]{:S(2)}, u32[]{:S(2)}) collective-permute-start(f32[64,32]{0,1:T(8,128)S(1)} %copy.39), channel_id=1, source_target_pairs={{28,0},{32,4},{36,8},{40,12},{44,16},{48,20},{52,24},{56,28},{60,3... | collective-permute-start | bytes 24584 | tf_op jit(solution)/shard_map/ppermute | solution.py:19
  571.5 9.1 %collective-permute-start.14 = (f32[64,32]{0,1:T(8,128)S(1)}, f32[64,32]{0,1:T(8,128)S(1)}, u32[]{:S(2)}, u32[]{:S(2)}) collective-permute-start(f32[64,32]{0,1:T(8,128)S(1)} %copy.40), channel_id=1, source_target_pairs={{32,0},{36,4},{40,8},{44,12},{48,16},{52,20},{56,24},{60,28},{64,3... | collective-permute-start | bytes 24584 | tf_op jit(solution)/shard_map/ppermute | solution.py:19
  572.8 10.6 %collective-permute-start.15 = (f32[64,32]{0,1:T(8,128)S(1)}, f32[64,32]{0,1:T(8,128)S(1)}, u32[]{:S(2)}, u32[]{:S(2)}) collective-permute-start(f32[64,32]{0,1:T(8,128)S(1)} %copy.41), channel_id=1, source_target_pairs={{36,0},{40,4},{44,8},{48,12},{52,16},{56,20},{60,24},{64,28},{68,3... | collective-permute-start | bytes 24584 | tf_op jit(solution)/shard_map/ppermute | solution.py:19
Sparse Core Ops, SparseCore 0:
  97.7 33.6 reduce-scatter.3
Sparse Core Ops, SparseCore 1:
  198.2 350.6 all-reduce.1
where the time goes:
time: 598 us; the launch traced here: 594 us
  waiting for transfers between devices  343 us (57%)
  other arithmetic  80.9 us (14%)
  starting transfers between devices  71.8 us (12%)
  local copies, waits for them, and re-layouts  56.9 us (10%)
  matrix products  15.9 us (3%)
  between operations  15.9 us (3%)
  blocking collectives  9.5 us (2%)
    psum x1, waiting for transfers between devices, body(): lax.psum(wgrad_local, 'dom') * (1.0 / math.sqrt(local_vox * n_dom))  333 us
    ppermute x16, starting transfers between devices, from_behind(): return lax.ppermute(block, axis, route)  71.7 us
    scatter-add x1, other arithmetic, spread_table(): jnp.zeros((rows_here, total_cols), jnp.float32).at[:, nbr_flat].add(spread)  56.4 us
    gather x2, local copies, waits for them, and re-layouts, body(): segment[:, nbr_index]  37.8 us
    select_n x1, other arithmetic, spread_table(): spread = jnp.where(valid_flat[None, :], spread, 0.0)  12.3 us
  transfers between devices with their start and end apart: 18, of which 4 were waited for; matrix products, arithmetic and copies ran while one was open for 10% of the time, Pallas kernels for 0%

commit v1 on v0

v1 whole, which is shorter than its diff:
```python
import math

import jax
import jax.numpy as jnp
from jax import lax
from jax.experimental import pallas as pl
from jax.experimental.pallas import tpu as pltpu
from jax.sharding import PartitionSpec as P

C = 256
KVOL = 27
CAP = 32
SUB = 4
NX = 4
NZ = 16
DOM = 2 * NX * NZ
SHARE = C // SUB
VOX = 384
HALO = 8 * CAP
COLS = VOX + HALO
GRID_Y = 8
DIRECTIONS = ((-1, -1), (-1, 0), (-1, 1), (0, -1), (0, 1), (1, -1), (1, 0), (1, 1))
HOPS = tuple(dx * GRID_Y + dy for dx, dy in DIRECTIONS)
CHUNKS = ((0, 15), (15, 27))
UNROLL = 3
STEPS = 128.0
TOP = 32000.0
MESH = pl.DeviceIdType.MESH
F32 = jnp.float32
BF16 = jnp.bfloat16
I16 = jnp.int16


def dot(a, b, dims):
    return lax.dot_general(a, b, (dims, ((), ())), preferred_element_type=F32)


NN = ((1,), (0,))
NT = ((1,), (1,))
TN = ((0,), (0,))


def encode(tiles, n):
    row = lax.broadcasted_iota(jnp.int32, tiles.shape, tiles.ndim - 2)
    tiles = jnp.where(row < n, tiles, 0.0)
    top = jnp.max(jnp.abs(tiles), axis=-2, keepdims=True)
    level = jnp.ceil(jnp.log2(jnp.maximum(top, 1e-33)) * STEPS)
    codes = jnp.round(tiles * (jnp.exp2(level * (-1.0 / STEPS)) * TOP))
    return jnp.where(row == n, level, codes).astype(jnp.int32).astype(I16)


def decode(codes, n):
    values = codes.astype(jnp.int32).astype(F32)
    level = values[..., n : n + 1, :]
    return values * (jnp.exp2(level * (1.0 / STEPS)) * (1.0 / TOP))


def kernel(
    feats, weight, grad_out, neighbors, send_rows, send_counts,
    out_feats, grad_feats, codes,
    nbr_t, onehot, picked, spread_hi, spread_lo, share_all, halo_out, halo_in, halo_all,
    table, wg, pair_in, x_out, x_in, x_sum, z_out, z_in, tg, tg_in, back_out, back_in,
    send, recv,
):
    me = lax.axis_index("dom")
    sub = lax.axis_index("sub")
    core = lax.rem(me, 2)
    z = lax.rem(me // 2, NZ)
    x = me // (2 * NZ)

    def wrap(i):
        return lax.rem(i + DOM, DOM)

    def at(xx, zz, cc):
        return (xx * NZ + zz) * 2 + cc

    twin = at(x, z, 1 - core)

    def x_peer(d):
        return lax.rem(x + d, NX)

    def z_peer(d):
        return lax.rem(z + d, NZ)

    def y_peer(d):
        return lax.rem(sub + d, SUB)

    slots = {}

    def copy(name, index, src, dst, device):
        base = slots[name]
        return pltpu.make_async_remote_copy(
            src_ref=src, dst_ref=dst, send_sem=send.at[base + index], recv_sem=recv.at[base + index],
            device_id=device, device_id_type=MESH,
        )

    for base, name in enumerate(("share", "fwd", "tg")):
        slots[name] = 3 * base
    slots["halo"], slots["back"] = 9, 17
    slots["pair"], slots["gpair"] = 25, 27
    slots["x"], slots["gx"] = 29, 35
    slots["z"], slots["gz"] = 41, 73

    barrier = pltpu.get_barrier_semaphore()
    peers = [(me, y_peer(d)) for d in range(1, SUB)]
    peers += [(wrap(me + hop), sub) for hop in HOPS]
    peers += [(twin, sub)]
    peers += [(at(x_peer(d), z, core), sub) for d in range(1, NX)]
    with jax.named_scope("barrier_signals"):
        for peer in peers:
            pl.semaphore_signal(barrier, inc=1, device_id=peer, device_id_type=MESH)

        @pl.loop(1, NZ)
        def _(d):
            pl.semaphore_signal(barrier, inc=1, device_id=(at(x, z_peer(d), core), sub), device_id_type=MESH)

    with jax.named_scope("boundary_tiles"):
        lane = lax.broadcasted_iota(jnp.int32, (1, HALO), 1)
        mine = send_counts[...]
        mine = jnp.where(lax.broadcasted_iota(jnp.int32, (8, DOM), 1) == me, mine, 0).astype(F32)
        mine = jnp.sum(mine, axis=1, keepdims=True).astype(jnp.int32)
        count = jnp.zeros((1, HALO), jnp.int32)
        for n in range(8):
            count = jnp.where(lane // CAP == n, mine[n : n + 1, :], count)
        rows = jnp.where(lane % CAP < count, send_rows[...], -1)
        pick = (lax.broadcasted_iota(jnp.int32, (VOX, HALO), 0) == rows).astype(F32).astype(BF16)
        outgoing = dot(feats[...], pick, NN).T.reshape(8, 2, 16, SHARE)
        halo_out[...] = jnp.concatenate([outgoing[:, 0], outgoing[:, 1]], axis=-1).astype(BF16)

    with jax.named_scope("barrier_wait"):
        pl.semaphore_wait(barrier, len(peers) + NZ - 1)

    def share_copy(d):
        return copy("share", d - 1, feats, share_all.at[sub], (me, y_peer(d)))

    def halo_copy(n):
        return copy("halo", n, halo_out.at[n], halo_in.at[n], (wrap(me + HOPS[n]), sub))

    def fwd_copy(d):
        return copy("fwd", d - 1, halo_in, halo_all.at[sub], (me, y_peer(d)))

    with jax.named_scope("first_sends"):
        for n in range(8):
            halo_copy(n).start()
        for d in range(1, SUB):
            share_copy(d).start()
        share_all[sub] = feats[...]

    with jax.named_scope("transpose_maps"):
        nbr_t[...] = jnp.concatenate(
            [neighbors[...], jnp.zeros((128 - KVOL, VOX), jnp.int32)], axis=0
        ).T
        col = lax.broadcasted_iota(jnp.int32, (1, COLS), 1)
        r = col - VOX
        slot = jnp.where(col < VOX, col, VOX + ((r % 128) // 16) * CAP + (r // 128) * 16 + r % 16)
        spread_hi[KVOL] = jnp.zeros((SHARE, COLS), BF16)
        spread_lo[KVOL] = jnp.zeros((SHARE, COLS), BF16)

    with jax.named_scope("onehot_and_spread"):
        @pl.loop(0, KVOL // UNROLL)
        def _(g):
            now = nbr_t[...]
            nbr_t[...] = pltpu.roll(now, 128 - UNROLL, 1)
            for j in range(UNROLL):
                k = g * UNROLL + j
                hot = (now[:, j : j + 1] == slot).astype(F32).astype(BF16)
                onehot[k] = hot
                total = dot(grad_out[...], hot, NN)
                high = total.astype(BF16)
                spread_hi[k] = high
                spread_lo[k] = (total - high.astype(F32)).astype(BF16)

    with jax.named_scope("halo_arrival"):
        for n in range(8):
            halo_copy(n).wait_recv()
        for d in range(1, SUB):
            fwd_copy(d).start()
        halo_all[sub] = halo_in[...]

    with jax.named_scope("table_grad"):
        total = None
        for k in range(0, KVOL, 4):
            n = min(4, KVOL - k)
            w = weight[k : k + n].reshape(n * SHARE, C)
            for part in (spread_hi, spread_lo):
                term = dot(w, part[k : k + n].reshape(n * SHARE, COLS), TN)
                total = term if total is None else total + term
        tg[...] = total.reshape(SUB, SHARE, COLS)

    def tg_copy(d):
        return copy("tg", d - 1, tg.at[y_peer(d)], tg_in.at[d - 1], (me, y_peer(d)))

    with jax.named_scope("tg_sends"):
        for d in range(1, SUB):
            tg_copy(d).start()

    with jax.named_scope("table"):
        for d in range(1, SUB):
            share_copy(d).wait_recv()
        table[0:VOX] = share_all[...].reshape(C, VOX).T
        for d in range(1, SUB):
            fwd_copy(d).wait_recv()
        tiles = halo_all[...].reshape(SUB, 128, 128)
        for half in range(2):
            lanes = slice(half * SHARE, (half + 1) * SHARE)
            table[VOX + half * 128 : VOX + (half + 1) * 128] = jnp.concatenate(
                [tiles[s][:, lanes] for s in range(SUB)], axis=1
            )

    def pair_copy(c):
        return copy("pair", c, wg.at[c, 1 - core], pair_in.at[c], (twin, sub))

    def x_copy(c, d):
        return copy("x", 3 * c + d - 1, x_out.at[c, x_peer(d)], x_in.at[c, d - 1], (at(x_peer(d), z, core), sub))

    def own_tile(zz):
        return pl.ds(pl.multiple_of(zz * 16, 16), 16)

    def z_copy(c, d):
        return copy("z", 16 * c + d - 1, z_out.at[c, own_tile(z_peer(d))], z_in.at[c, d - 1], (at(x, z_peer(d), core), sub))

    def gz_copy(c, d):
        ref = codes.at[c, core, x, own_tile(z)]
        return copy("gz", 16 * c + d - 1, ref, ref, (at(x, z_peer(d), core), sub))

    def gz_arrival(c, d):
        ref = codes.at[c, core, x, own_tile(z_peer(NZ - d))]
        return copy("gz", 16 * c + d - 1, ref, ref, (at(x, z_peer(d), core), sub))

    def gx_copy(c, d):
        ref = codes.at[c, core, x]
        return copy("gx", 3 * c + d - 1, ref, ref, (at(x_peer(d), z, core), sub))

    def gx_arrival(c, d):
        ref = codes.at[c, core, x_peer(NX - d)]
        return copy("gx", 3 * c + d - 1, ref, ref, (at(x_peer(d), z, core), sub))

    def gpair_copy(c):
        ref = codes.at[c, core]
        return copy("gpair", c, ref, ref, (twin, sub))

    def gpair_arrival(c):
        ref = codes.at[c, 1 - core]
        return copy("gpair", c, ref, ref, (twin, sub))

    def gather(c, first, last):
        lo = CHUNKS[c][0]

        @pl.loop(first // UNROLL, last // UNROLL)
        def _(g):
            k0 = g * UNROLL
            hot = onehot[pl.ds(k0, UNROLL)].reshape(UNROLL * VOX, COLS)
            got = dot(hot, table[...], NN).astype(BF16).reshape(UNROLL, VOX, C)
            picked[pl.ds(k0, UNROLL)] = got
            for j in range(UNROLL):
                fresh = dot(grad_out[...], got[j], NN)
                for cc in range(2):
                    for xx in range(NX):
                        r0, l0 = cc * 32 + (xx // 2) * 16, (xx % 2) * 128
                        wg[c, cc, xx, pl.ds(k0 + j - lo, 16, stride=16), :] = fresh[r0 : r0 + 16, l0 : l0 + 128]

    def pair_to_x(c):
        lo, hi = CHUNKS[c]
        pair_copy(c).wait_recv()
        for xx in range(NX):
            both = wg[c, core, xx] + pair_in[c, xx]
            x_out[c, xx] = encode(both.reshape(16, 16, 128), hi - lo).reshape(256, 128)
        for d in range(1, NX):
            x_copy(c, d).start()

    def x_to_z(c):
        lo, hi = CHUNKS[c]
        for d in range(1, NX):
            x_copy(c, d).wait_recv()
        total = (wg[c, core, x] + pair_in[c, x]).reshape(16, 16, 128)
        for d in range(1, NX):
            total = total + decode(x_in[c, d - 1].reshape(16, 16, 128), hi - lo)
        x_sum[c] = total.reshape(256, 128)
        z_out[c] = encode(total, hi - lo).reshape(256, 128)

        @pl.loop(1, NZ)
        def _(d):
            z_copy(c, d).start()

    with jax.named_scope("wg_rows"):
        for c, (lo, hi) in enumerate(CHUNKS):
            for row in range(hi - lo, 16):
                for cc in range(2):
                    for xx in range(NX):
                        wg[c, cc, xx, pl.ds(row, 16, stride=16), :] = jnp.zeros((16, 128), F32)

    with jax.named_scope("gather_a"):
        gather(0, 0, 15)
    with jax.named_scope("pair_a"):
        pair_copy(0).start()
    with jax.named_scope("gather_b"):
        gather(1, 15, 21)
    with jax.named_scope("pair_to_x_a"):
        pair_to_x(0)
    with jax.named_scope("gather_c"):
        gather(1, 21, 27)
    with jax.named_scope("pair_b"):
        pair_copy(1).start()

    with jax.named_scope("tg_sum"):
        for d in range(1, SUB):
            tg_copy(d).wait_recv()
        mine_tg = tg[sub] + tg_in[0] + tg_in[1] + tg_in[2]
        tail = mine_tg[:, VOX:].T
        back_out[...] = jnp.concatenate([tail[:128], tail[128:]], axis=1).reshape(8, 16, 128)

    def back_copy(n):
        return copy("back", n, back_out.at[n], back_in.at[n], (wrap(me - HOPS[n]), sub))

    with jax.named_scope("back_sends"):
        for n in range(8):
            back_copy(n).start()

    with jax.named_scope("x_to_z_a"):
        x_to_z(0)
    with jax.named_scope("pair_to_x_b"):
        pair_to_x(1)

    with jax.named_scope("out_feats"):
        def out_step(g, acc):
            for j in range(UNROLL):
                acc = acc + dot(weight[g * UNROLL + j], picked[g * UNROLL + j], NT)
            return acc

        out_feats[...] = lax.fori_loop(0, KVOL // UNROLL, out_step, jnp.zeros((SHARE, VOX), F32)).astype(BF16)

    with jax.named_scope("x_to_z_b"):
        x_to_z(1)

    with jax.named_scope("grad_feats"):
        for n in range(8):
            back_copy(n).wait_recv()
        back = back_in[...]
        back = jnp.concatenate([back[:, :, :SHARE][:, None], back[:, :, SHARE:][:, None]], axis=1)
        back = back.reshape(HALO, SHARE).T
        back_hi = back.astype(BF16)
        back_lo = (back - back_hi.astype(F32)).astype(BF16)
        grad_feats[...] = mine_tg[:, :VOX] + dot(back_hi, pick, NT) + dot(back_lo, pick, NT)

    def z_reduce(c):
        lo, hi = CHUNKS[c]

        @pl.loop(1, NZ)
        def _(d):
            z_copy(c, d).wait_recv()

        total = x_sum[c, own_tile(z)] + jnp.sum(decode(z_in[c], hi - lo), axis=0)
        scaled = total * (1.0 / math.sqrt(VOX * DOM))
        codes[c, core, x, own_tile(z)] = encode(scaled, hi - lo)

        @pl.loop(1, NZ)
        def _(d):
            gz_copy(c, d).start()

    def z_to_x(c):
        @pl.loop(1, NZ)
        def _(d):
            gz_arrival(c, d).wait_recv()

        for d in range(1, NX):
            gx_copy(c, d).start()

    def x_to_pair(c):
        for d in range(1, NX):
            gx_arrival(c, d).wait_recv()
        gpair_copy(c).start()

    with jax.named_scope("z_reduce_a"):
        z_reduce(0)
    with jax.named_scope("z_reduce_b"):
        z_reduce(1)
    with jax.named_scope("z_back"):
        z_to_x(0)
        z_to_x(1)
    with jax.named_scope("x_back"):
        x_to_pair(0)
        x_to_pair(1)
    with jax.named_scope("pair_back"):
        gpair_arrival(0).wait_recv()
        gpair_arrival(1).wait_recv()

    with jax.named_scope("drain"):
        for d in range(1, SUB):
            share_copy(d).wait_send()
            fwd_copy(d).wait_send()
            tg_copy(d).wait_send()
        for n in range(8):
            halo_copy(n).wait_send()
            back_copy(n).wait_send()
        for c in range(2):
            pair_copy(c).wait_send()
            gpair_copy(c).wait_send()
            for d in range(1, NX):
                x_copy(c, d).wait_send()
                gx_copy(c, d).wait_send()

            @pl.loop(1, NZ)
            def _(d):
                z_copy(c, d).wait_send()
                gz_copy(c, d).wait_send()


def finish(codes, out_in, feats_in, out_feats, grad_feats, grad_weight):
    out_feats[...] = out_in[...]
    grad_feats[...] = feats_in[...]
    for c, (lo, hi) in enumerate(CHUNKS):
        for cc in range(2):
            for xx in range(NX):
                values = decode(codes[c, cc, xx].reshape(16, 16, 128), hi - lo)
                r0, l0 = cc * 32 + (xx // 2) * 16, (xx % 2) * 128
                values = jnp.swapaxes(values, 0, 1)
                grad_weight[lo:hi, r0 : r0 + 16, l0 : l0 + 128] = values[: hi - lo]


def body(feats, weight, grad_out, neighbors, send_rows, send_counts):
    vmem = pl.BlockSpec(memory_space=pltpu.VMEM)
    out_feats, grad_feats, codes = pl.pallas_call(
        kernel,
        out_shape=(
            jax.ShapeDtypeStruct((SHARE, VOX), BF16),
            jax.ShapeDtypeStruct((SHARE, VOX), F32),
            jax.ShapeDtypeStruct((2, 2, NX, 256, 128), I16),
        ),
        in_specs=[vmem] * 6,
        out_specs=[vmem] * 3,
        scratch_shapes=[
            pltpu.VMEM((VOX, 128), jnp.int32),
            pltpu.VMEM((KVOL, VOX, COLS), BF16),
            pltpu.VMEM((KVOL, VOX, C), BF16),
            pltpu.VMEM((KVOL + 1, SHARE, COLS), BF16),
            pltpu.VMEM((KVOL + 1, SHARE, COLS), BF16),
            pltpu.VMEM((SUB, SHARE, VOX), BF16),
            pltpu.VMEM((8, 16, 128), BF16),
            pltpu.VMEM((8, 16, 128), BF16),
            pltpu.VMEM((SUB, 8, 16, 128), BF16),
            pltpu.VMEM((COLS, C), BF16),
            pltpu.VMEM((2, 2, NX, 256, 128), F32),
            pltpu.VMEM((2, NX, 256, 128), F32),
            pltpu.VMEM((2, NX, 256, 128), I16),
            pltpu.VMEM((2, NX - 1, 256, 128), I16),
            pltpu.VMEM((2, 256, 128), F32),
            pltpu.VMEM((2, 256, 128), I16),
            pltpu.VMEM((2, NZ - 1, 16, 128), I16),
            pltpu.VMEM((SUB, SHARE, COLS), F32),
            pltpu.VMEM((SUB - 1, SHARE, COLS), F32),
            pltpu.VMEM((8, 16, 128), F32),
            pltpu.VMEM((8, 16, 128), F32),
            pltpu.SemaphoreType.DMA((105,)),
            pltpu.SemaphoreType.DMA((105,)),
        ],
        compiler_params=pltpu.CompilerParams(
            collective_id=0, has_side_effects=True, vmem_limit_bytes=56 * 1024 * 1024
        ),
    )(feats, weight, grad_out, neighbors, send_rows, send_counts.T)
    return pl.pallas_call(
        finish,
        out_shape=(
            jax.ShapeDtypeStruct((SHARE, VOX), BF16),
            jax.ShapeDtypeStruct((SHARE, VOX), F32),
            jax.ShapeDtypeStruct((KVOL, SHARE, C), F32),
        ),
        in_specs=[vmem] * 3,
        out_specs=[vmem] * 3,
        compiler_params=pltpu.CompilerParams(vmem_limit_bytes=32 * 1024 * 1024),
    )(codes, out_feats, grad_feats)


def solution(mesh):
    in_specs = (
        P("sub", "dom"),
        P(None, "sub", None),
        P("sub", "dom"),
        P(None, "dom"),
        P("dom", None),
        P(),
    )
    out_specs = (P("sub", "dom"), P("sub", "dom"), P(None, "sub", None))
    return jax.shard_map(body, mesh=mesh, in_specs=in_specs, out_specs=out_specs, check_vma=False)
```

time: 598 us -> 78.9 us (0.13)
  waiting for transfers between devices: 343 us -> 0 us
  other arithmetic: 80.9 us -> 0 us
  Pallas kernels: 0 us -> 75.1 us
  starting transfers between devices: 71.8 us -> 0 us
  local copies, waits for them, and re-layouts: 56.9 us -> 2.91 us
  matrix products: 15.9 us -> 0 us
  between operations: 15.9 us -> 0.65 us
  blocking collectives: 9.5 us -> 0 us
    psum x1 -> x0, waiting for transfers between devices: 333 us -> none  [body(): lax.psum(wgrad_local, 'dom') * (1.0 / math.sqrt(local_vox * n_dom))]
    pallas_call x0 -> x2, Pallas kernels: none -> 75.1 us  [the longest x1 73.2 us: body(): pl.pallas_call(kernel, out_shape=(jax.ShapeDtypeStruct((SHARE, VOX), BF16...]
    ppermute x16 -> x0, starting transfers between devices: 71.7 us -> none  [from_behind(): return lax.ppermute(block, axis, route)]
    scatter-add x2 -> x0, other arithmetic: 58.5 us -> none  [the longest x1 56.4 us: spread_table(): jnp.zeros((rows_here, total_cols), jnp.float32).at[:, nbr_flat].add(spread)]
    gather x4 -> x0, local copies, waits for them, and re-layouts: 39.3 us -> none  [the longest x2 37.8 us: body(): segment[:, nbr_index]]
    dot_general x3 -> x0, matrix products: 15.9 us -> none  [the longest x1 6.28 us: spread_table(): lax.dot_general(w_part, cotangent, (((1,), (0,)), ((), ())), preferred_el...]
    select_n x4 -> x0, other arithmetic: 12.5 us -> none  [the longest x1 12.3 us: spread_table(): spread = jnp.where(valid_flat[None, :], spread, 0.0)]
    transpose x1 -> x0, local copies, waits for them, and re-layouts: 11.6 us -> none  [spread_table(): spread = jnp.transpose(spread, (1, 0, 2))]
  transfers between devices with their start and end apart: 18 -> 0, of which waited for: 4 -> 0; matrix products, arithmetic and copies ran while one was open for 10% -> 0% of each run, Pallas kernels for 0% -> 0%
where the time goes in v1:
time: 78.9 us; the launch traced here: 78.6 us
  Pallas kernels  75.1 us (95%)
  local copies, waits for them, and re-layouts  2.91 us (4%)
    pallas_call x1, Pallas kernels, body(): pl.pallas_call(kernel, out_shape=(jax.ShapeDtypeStruct((SHARE, VOX), BF16...  73.2 us
    unnamed x6, local copies, waits for them, and re-layouts  2.91 us
    pallas_call x1, Pallas kernels, body(): pl.pallas_call(finish, out_shape=(jax.ShapeDtypeStruct((SHARE, VOX), BF16...  1.86 us

profile of v1, /device:TPU:1, one launch (start us, length us, event | category | flops | bytes accessed | tf_op | source)
XLA Modules:
  0.0 78.6 jit_solution(10156220512619341441)
XLA Ops:
  0.6 73.2 %shard_map.85 = (bf16[64,384]{1,0:T(8,128)(2,1)}, f32[64,384]{1,0:T(8,128)}, s16[2,2,4,256,128]{4,3,2,1,0:T(8,128)(2,1)}) custom-call(bf16[64,384]{1,0:T(8,128)(2,1)} %feats.1, bf16[27,64,256]{2,1,0:T(8,128)(2,1)} %weight.1, bf16[64,384]{1,0:T(8,128)(2,1)} %grad_out.1, s32[27,384]{1,0:T(8,128)} %neighbors.1, s32[1,256]{1,0:T(1,128)} %send_rows.1, ...), custom_call_target="tpu_custom_call" | custom-call | tf_op jit(solution)/shard_map/pallas_call | solution.py:422
  73.9 0.0 copy-start
  73.9 1.2 %copy-done = s16[2,2,4,256,128]{4,3,2,1,0:T(8,128)(2,1)S(1)} copy-done((s16[2,2,4,256,128]{4,3,2,1,0:T(8,128)(2,1)S(1)}, s16[2,2,4,256,128]{4,3,2,1,0:T(8,128)(2,1)}, u32[]{:S(2)}) %copy-start) | copy-done | bytes 1048600
  75.1 0.0 copy-start.1
  75.1 0.9 %copy-done.1 = f32[64,384]{1,0:T(8,128)S(1)} copy-done((f32[64,384]{1,0:T(8,128)S(1)}, f32[64,384]{1,0:T(8,128)}, u32[]{:S(2)}) %copy-start.1) | copy-done | bytes 98328
  76.0 0.0 copy-start.2
  76.0 0.8 %copy-done.2 = bf16[64,384]{1,0:T(8,128)(2,1)S(1)} copy-done((bf16[64,384]{1,0:T(8,128)(2,1)S(1)}, bf16[64,384]{1,0:T(8,128)(2,1)}, u32[]{:S(2)}) %copy-start.2) | copy-done | bytes 49176
  76.8 1.9 %shard_map.86 = (bf16[64,384]{1,0:T(8,128)(2,1)}, f32[64,384]{1,0:T(8,128)}, f32[27,64,256]{2,1,0:T(8,128)}) custom-call(s16[2,2,4,256,128]{4,3,2,1,0:T(8,128)(2,1)S(1)} %copy-done, bf16[64,384]{1,0:T(8,128)(2,1)S(1)} %copy-done.2, f32[64,384]{1,0:T(8,128)S(1)} %copy-done.1), custom_call_target="tpu_custom_call" | custom-call | tf_op jit(solution)/shard_map/pallas_call | solution.py:460
Async XLA Ops:
  73.9 1.2 %copy-start = (s16[2,2,4,256,128]{4,3,2,1,0:T(8,128)(2,1)S(1)}, s16[2,2,4,256,128]{4,3,2,1,0:T(8,128)(2,1)}, u32[]{:S(2)}) copy-start(s16[2,2,4,256,128]{4,3,2,1,0:T(8,128)(2,1)} %get-tuple-element.6.codes) | copy-start | bytes 3145732
  75.1 0.9 %copy-start.1 = (f32[64,384]{1,0:T(8,128)S(1)}, f32[64,384]{1,0:T(8,128)}, u32[]{:S(2)}) copy-start(f32[64,384]{1,0:T(8,128)} %get-tuple-element.8.feats_in) | copy-start | bytes 294916
  76.0 0.8 %copy-start.2 = (bf16[64,384]{1,0:T(8,128)(2,1)S(1)}, bf16[64,384]{1,0:T(8,128)(2,1)}, u32[]{:S(2)}) copy-start(bf16[64,384]{1,0:T(8,128)(2,1)} %get-tuple-element.7.out_in) | copy-start | bytes 147460

commit v2 on v1

--- a/solution.py
+++ b/solution.py
@@ -153,22 +153,28 @@
         col = lax.broadcasted_iota(jnp.int32, (1, COLS), 1)
         r = col - VOX
         slot = jnp.where(col < VOX, col, VOX + ((r % 128) // 16) * CAP + (r // 128) * 16 + r % 16)
-        spread_hi[KVOL] = jnp.zeros((SHARE, COLS), BF16)
-        spread_lo[KVOL] = jnp.zeros((SHARE, COLS), BF16)
-
-    with jax.named_scope("onehot_and_spread"):
+
+    with jax.named_scope("onehot"):
         @pl.loop(0, KVOL // UNROLL)
         def _(g):
             now = nbr_t[...]
             nbr_t[...] = pltpu.roll(now, 128 - UNROLL, 1)
             for j in range(UNROLL):
-                k = g * UNROLL + j
-                hot = (now[:, j : j + 1] == slot).astype(F32).astype(BF16)
-                onehot[k] = hot
-                total = dot(grad_out[...], hot, NN)
-                high = total.astype(BF16)
-                spread_hi[k] = high
-                spread_lo[k] = (total - high.astype(F32)).astype(BF16)
+                onehot[g * UNROLL + j] = (now[:, j : j + 1] == slot).astype(F32).astype(BF16)
+
+    def gather_own(first, last):
+        @pl.loop(first // UNROLL, last // UNROLL)
+        def _(g):
+            hot = onehot[pl.ds(g * UNROLL, UNROLL), :, 0:VOX].reshape(UNROLL * VOX, VOX)
+            got = dot(hot, table[0:VOX], NN).astype(BF16)
+            picked[pl.ds(g * UNROLL, UNROLL)] = got.reshape(UNROLL, VOX, C)
+
+    with jax.named_scope("table_own"):
+        for d in range(1, SUB):
+            share_copy(d).wait_recv()
+        table[0:VOX] = share_all[...].reshape(C, VOX).T
+    with jax.named_scope("gather_own_a"):
+        gather_own(0, 15)
 
     with jax.named_scope("halo_arrival"):
         for n in range(8):
@@ -177,27 +183,10 @@
             fwd_copy(d).start()
         halo_all[sub] = halo_in[...]
 
-    with jax.named_scope("table_grad"):
-        total = None
-        for k in range(0, KVOL, 4):
-            n = min(4, KVOL - k)
-            w = weight[k : k + n].reshape(n * SHARE, C)
-            for part in (spread_hi, spread_lo):
-                term = dot(w, part[k : k + n].reshape(n * SHARE, COLS), TN)
-                total = term if total is None else total + term
-        tg[...] = total.reshape(SUB, SHARE, COLS)
-
-    def tg_copy(d):
-        return copy("tg", d - 1, tg.at[y_peer(d)], tg_in.at[d - 1], (me, y_peer(d)))
-
-    with jax.named_scope("tg_sends"):
-        for d in range(1, SUB):
-            tg_copy(d).start()
-
-    with jax.named_scope("table"):
-        for d in range(1, SUB):
-            share_copy(d).wait_recv()
-        table[0:VOX] = share_all[...].reshape(C, VOX).T
+    with jax.named_scope("gather_own_b"):
+        gather_own(15, 27)
+
+    with jax.named_scope("table_halo"):
         for d in range(1, SUB):
             fwd_copy(d).wait_recv()
         tiles = halo_all[...].reshape(SUB, 128, 128)
@@ -249,8 +238,9 @@
         @pl.loop(first // UNROLL, last // UNROLL)
         def _(g):
             k0 = g * UNROLL
-            hot = onehot[pl.ds(k0, UNROLL)].reshape(UNROLL * VOX, COLS)
-            got = dot(hot, table[...], NN).astype(BF16).reshape(UNROLL, VOX, C)
+            hot = onehot[pl.ds(k0, UNROLL), :, VOX:COLS].reshape(UNROLL * VOX, HALO)
+            got = dot(hot, table[VOX:COLS], NN).astype(BF16).reshape(UNROLL, VOX, C)
+            got = got + picked[pl.ds(k0, UNROLL)]
             picked[pl.ds(k0, UNROLL)] = got
             for j in range(UNROLL):
                 fresh = dot(grad_out[...], got[j], NN)
@@ -302,24 +292,71 @@
     with jax.named_scope("pair_b"):
         pair_copy(1).start()
 
-    with jax.named_scope("tg_sum"):
-        for d in range(1, SUB):
-            tg_copy(d).wait_recv()
-        mine_tg = tg[sub] + tg_in[0] + tg_in[1] + tg_in[2]
-        tail = mine_tg[:, VOX:].T
-        back_out[...] = jnp.concatenate([tail[:128], tail[128:]], axis=1).reshape(8, 16, 128)
-
-    def back_copy(n):
-        return copy("back", n, back_out.at[n], back_in.at[n], (wrap(me - HOPS[n]), sub))
-
-    with jax.named_scope("back_sends"):
-        for n in range(8):
-            back_copy(n).start()
-
     with jax.named_scope("x_to_z_a"):
         x_to_z(0)
     with jax.named_scope("pair_to_x_b"):
         pair_to_x(1)
+
+    with jax.named_scope("spread"):
+        @pl.loop(0, KVOL // UNROLL)
+        def _(g):
+            for j in range(UNROLL):
+                k = g * UNROLL + j
+                total = dot(grad_out[...], onehot[k], NN)
+                high = total.astype(BF16)
+                spread_hi[k] = high
+                spread_lo[k] = (total - high.astype(F32)).astype(BF16)
+
+    with jax.named_scope("table_grad"):
+        total = None
+        for k in range(0, KVOL, 4):
+            n = min(4, KVOL - k)
+            w = weight[k : k + n].reshape(n * SHARE, C)
+            for part in (spread_hi, spread_lo):
+                term = dot(w, part[k : k + n].reshape(n * SHARE, COLS), TN)
+                total = term if total is None else total + term
+        tg[...] = total.reshape(SUB, SHARE, COLS)
+
+    def tg_copy(d):
+        return copy("tg", d - 1, tg.at[y_peer(d)], tg_in.at[d - 1], (me, y_peer(d)))
+
+    with jax.named_scope("tg_sends"):
+        for d in range(1, SUB):
+            tg_copy(d).start()
+
+    with jax.named_scope("x_to_z_b"):
+        x_to_z(1)
+
+    def z_reduce(c):
+        lo, hi = CHUNKS[c]
+
+        @pl.loop(1, NZ)
+        def _(d):
+            z_copy(c, d).wait_recv()
+
+        total = x_sum[c, own_tile(z)] + jnp.sum(decode(z_in[c], hi - lo), axis=0)
+        scaled = total * (1.0 / math.sqrt(VOX * DOM))
+        codes[c, core, x, own_tile(z)] = encode(scaled, hi - lo)
+
+        @pl.loop(1, NZ)
+        def _(d):
+            gz_copy(c, d).start()
+
+    def z_to_x(c):
+        @pl.loop(1, NZ)
+        def _(d):
+            gz_arrival(c, d).wait_recv()
+
+        for d in range(1, NX):
+            gx_copy(c, d).start()
+
+    def x_to_pair(c):
+        for d in range(1, NX):
+            gx_arrival(c, d).wait_recv()
+        gpair_copy(c).start()
+
+    with jax.named_scope("z_reduce_a"):
+        z_reduce(0)
 
     with jax.named_scope("out_feats"):
         def out_step(g, acc):
@@ -329,8 +366,29 @@
 
         out_feats[...] = lax.fori_loop(0, KVOL // UNROLL, out_step, jnp.zeros((SHARE, VOX), F32)).astype(BF16)
 
-    with jax.named_scope("x_to_z_b"):
-        x_to_z(1)
+    with jax.named_scope("z_reduce_b"):
+        z_reduce(1)
+
+    with jax.named_scope("tg_sum"):
+        for d in range(1, SUB):
+            tg_copy(d).wait_recv()
+        mine_tg = tg[sub] + tg_in[0] + tg_in[1] + tg_in[2]
+        tail = mine_tg[:, VOX:].T
+        back_out[...] = jnp.concatenate([tail[:128], tail[128:]], axis=1).reshape(8, 16, 128)
+
+    def back_copy(n):
+        return copy("back", n, back_out.at[n], back_in.at[n], (wrap(me - HOPS[n]), sub))
+
+    with jax.named_scope("back_sends"):
+        for n in range(8):
+            back_copy(n).start()
+
+    with jax.named_scope("z_back"):
+        z_to_x(0)
+        z_to_x(1)
+    with jax.named_scope("x_back"):
+        x_to_pair(0)
+        x_to_pair(1)
 
     with jax.named_scope("grad_feats"):
         for n in range(8):
@@ -342,44 +400,6 @@
         back_lo = (back - back_hi.astype(F32)).astype(BF16)
         grad_feats[...] = mine_tg[:, :VOX] + dot(back_hi, pick, NT) + dot(back_lo, pick, NT)
 
-    def z_reduce(c):
-        lo, hi = CHUNKS[c]
-
-        @pl.loop(1, NZ)
-        def _(d):
-            z_copy(c, d).wait_recv()
-
-        total = x_sum[c, own_tile(z)] + jnp.sum(decode(z_in[c], hi - lo), axis=0)
-        scaled = total * (1.0 / math.sqrt(VOX * DOM))
-        codes[c, core, x, own_tile(z)] = encode(scaled, hi - lo)
-
-        @pl.loop(1, NZ)
-        def _(d):
-            gz_copy(c, d).start()
-
-    def z_to_x(c):
-        @pl.loop(1, NZ)
-        def _(d):
-            gz_arrival(c, d).wait_recv()
-
-        for d in range(1, NX):
-            gx_copy(c, d).start()
-
-    def x_to_pair(c):
-        for d in range(1, NX):
-            gx_arrival(c, d).wait_recv()
-        gpair_copy(c).start()
-
-    with jax.named_scope("z_reduce_a"):
-        z_reduce(0)
-    with jax.named_scope("z_reduce_b"):
-        z_reduce(1)
-    with jax.named_scope("z_back"):
-        z_to_x(0)
-        z_to_x(1)
-    with jax.named_scope("x_back"):
-        x_to_pair(0)
-        x_to_pair(1)
     with jax.named_scope("pair_back"):
         gpair_arrival(0).wait_recv()
         gpair_arrival(1).wait_recv()
@@ -466,7 +486,7 @@
         ),
         in_specs=[vmem] * 3,
         out_specs=[vmem] * 3,
-        compiler_params=pltpu.CompilerParams(vmem_limit_bytes=32 * 1024 * 1024),
+        compiler_params=pltpu.CompilerParams(vmem_limit_bytes=60 * 1024 * 1024),
     )(codes, out_feats, grad_feats)
 
 

time: 78.9 us -> 77.7 us (0.985)
  local copies, waits for them, and re-layouts: 2.91 us -> 0 us
  Pallas kernels: 75.1 us -> 76.9 us
    unnamed x6 -> x0, local copies, waits for them, and re-layouts: 2.91 us -> none
    pallas_call x1, Pallas kernels: 1.86 us -> 3.12 us  [body(): pl.pallas_call(finish, out_shape=(jax.ShapeDtypeStruct((SHARE, VOX), BF16...]
where the time goes in v2:
time: 77.7 us; the launch traced here: 77.5 us
  Pallas kernels  76.9 us (99%)
    pallas_call x1, Pallas kernels, body(): pl.pallas_call(kernel, out_shape=(jax.ShapeDtypeStruct((SHARE, VOX), BF16...  73.8 us
    pallas_call x1, Pallas kernels, body(): pl.pallas_call(finish, out_shape=(jax.ShapeDtypeStruct((SHARE, VOX), BF16...  3.12 us

profile of v2, /device:TPU:1, one launch (start us, length us, event | category | flops | bytes accessed | tf_op | source)
XLA Modules:
  0.0 77.5 jit_solution(13336673704158077560)
XLA Ops:
  0.6 73.8 %shard_map.85 = (bf16[64,384]{1,0:T(8,128)(2,1)}, f32[64,384]{1,0:T(8,128)}, s16[2,2,4,256,128]{4,3,2,1,0:T(8,128)(2,1)}) custom-call(bf16[64,384]{1,0:T(8,128)(2,1)} %feats.1, bf16[27,64,256]{2,1,0:T(8,128)(2,1)} %weight.1, bf16[64,384]{1,0:T(8,128)(2,1)} %grad_out.1, s32[27,384]{1,0:T(8,128)} %neighbors.1, s32[1,256]{1,0:T(1,128)} %send_rows.1, ...), custom_call_target="tpu_custom_call" | custom-call | tf_op jit(solution)/shard_map/pallas_call | solution.py:442
  74.4 3.1 %shard_map.86 = (bf16[64,384]{1,0:T(8,128)(2,1)}, f32[64,384]{1,0:T(8,128)}, f32[27,64,256]{2,1,0:T(8,128)}) custom-call(s16[2,2,4,256,128]{4,3,2,1,0:T(8,128)(2,1)} %get-tuple-element.6.codes, bf16[64,384]{1,0:T(8,128)(2,1)} %get-tuple-element.7.out_in, f32[64,384]{1,0:T(8,128)} %get-tuple-element.8.feats_in), custom_call_target="tpu_custom_call" | custom-call | tf_op jit(solution)/shard_map/pallas_call | solution.py:480

commit v3 on v2

--- a/solution.py
+++ b/solution.py
@@ -56,11 +56,12 @@
 
 
 def kernel(
-    feats, weight, grad_out, neighbors, send_rows, send_counts,
-    out_feats, grad_feats, codes,
+    feats_hbm, weight_hbm, grad_out_hbm, neighbors_hbm, send_rows_hbm, send_counts_hbm,
+    out_feats_hbm, grad_feats_hbm, codes_hbm,
+    feats, weight, grad_out, neighbors, send_rows, send_counts, out_feats, grad_feats, codes,
     nbr_t, onehot, picked, spread_hi, spread_lo, share_all, halo_out, halo_in, halo_all,
     table, wg, pair_in, x_out, x_in, x_sum, z_out, z_in, tg, tg_in, back_out, back_in,
-    send, recv,
+    send, recv, local,
 ):
     me = lax.axis_index("dom")
     sub = lax.axis_index("sub")
@@ -114,7 +115,25 @@
         def _(d):
             pl.semaphore_signal(barrier, inc=1, device_id=(at(x, z_peer(d), core), sub), device_id_type=MESH)
 
+    def load(i):
+        pairs = (
+            (send_counts_hbm, send_counts), (send_rows_hbm, send_rows), (feats_hbm, feats),
+            (neighbors_hbm, neighbors), (grad_out_hbm, grad_out), (weight_hbm, weight),
+        )
+        return pltpu.make_async_copy(pairs[i][0], pairs[i][1], local.at[i])
+
+    def store(i):
+        pairs = [(out_feats, out_feats_hbm), (grad_feats, grad_feats_hbm)]
+        pairs += [(codes.at[c, half], codes_hbm.at[c, half]) for c in range(2) for half in (core, 1 - core)]
+        return pltpu.make_async_copy(pairs[i][0], pairs[i][1], local.at[6 + i])
+
+    with jax.named_scope("loads"):
+        for i in range(6):
+            load(i).start()
+
     with jax.named_scope("boundary_tiles"):
+        for i in range(3):
+            load(i).wait()
         lane = lax.broadcasted_iota(jnp.int32, (1, HALO), 1)
         mine = send_counts[...]
         mine = jnp.where(lax.broadcasted_iota(jnp.int32, (8, DOM), 1) == me, mine, 0).astype(F32)
@@ -147,6 +166,8 @@
         share_all[sub] = feats[...]
 
     with jax.named_scope("transpose_maps"):
+        for i in (3, 4, 5):
+            load(i).wait()
         nbr_t[...] = jnp.concatenate(
             [neighbors[...], jnp.zeros((128 - KVOL, VOX), jnp.int32)], axis=0
         ).T
@@ -292,8 +313,6 @@
     with jax.named_scope("pair_b"):
         pair_copy(1).start()
 
-    with jax.named_scope("x_to_z_a"):
-        x_to_z(0)
     with jax.named_scope("pair_to_x_b"):
         pair_to_x(1)
 
@@ -307,6 +326,9 @@
                 spread_hi[k] = high
                 spread_lo[k] = (total - high.astype(F32)).astype(BF16)
 
+    with jax.named_scope("x_to_z_a"):
+        x_to_z(0)
+
     with jax.named_scope("table_grad"):
         total = None
         for k in range(0, KVOL, 4):
@@ -354,6 +376,7 @@
         for d in range(1, NX):
             gx_arrival(c, d).wait_recv()
         gpair_copy(c).start()
+        store(2 + 2 * c).start()
 
     with jax.named_scope("z_reduce_a"):
         z_reduce(0)
@@ -365,6 +388,7 @@
             return acc
 
         out_feats[...] = lax.fori_loop(0, KVOL // UNROLL, out_step, jnp.zeros((SHARE, VOX), F32)).astype(BF16)
+        store(0).start()
 
     with jax.named_scope("z_reduce_b"):
         z_reduce(1)
@@ -399,10 +423,12 @@
         back_hi = back.astype(BF16)
         back_lo = (back - back_hi.astype(F32)).astype(BF16)
         grad_feats[...] = mine_tg[:, :VOX] + dot(back_hi, pick, NT) + dot(back_lo, pick, NT)
+        store(1).start()
 
     with jax.named_scope("pair_back"):
-        gpair_arrival(0).wait_recv()
-        gpair_arrival(1).wait_recv()
+        for c in range(2):
+            gpair_arrival(c).wait_recv()
+            store(3 + 2 * c).start()
 
     with jax.named_scope("drain"):
         for d in range(1, SUB):
@@ -423,22 +449,48 @@
             def _(d):
                 z_copy(c, d).wait_send()
                 gz_copy(c, d).wait_send()
-
-
-def finish(codes, out_in, feats_in, out_feats, grad_feats, grad_weight):
-    out_feats[...] = out_in[...]
-    grad_feats[...] = feats_in[...]
-    for c, (lo, hi) in enumerate(CHUNKS):
-        for cc in range(2):
-            for xx in range(NX):
-                values = decode(codes[c, cc, xx].reshape(16, 16, 128), hi - lo)
-                r0, l0 = cc * 32 + (xx // 2) * 16, (xx % 2) * 128
-                values = jnp.swapaxes(values, 0, 1)
-                grad_weight[lo:hi, r0 : r0 + 16, l0 : l0 + 128] = values[: hi - lo]
+    with jax.named_scope("stores"):
+        for i in range(6):
+            store(i).wait()
+
+
+def finish(codes_hbm, out_in, feats_in, out_feats, grad_feats, grad_weight_hbm, codes, grad_weight, arrive, leave):
+    parts = [(c, half) for c in range(2) for half in range(2)]
+
+    def load(i):
+        c, half = parts[i]
+        return pltpu.make_async_copy(codes_hbm.at[c, half], codes.at[c, half], arrive.at[i])
+
+    def store(i):
+        (lo, hi), r0 = CHUNKS[parts[i][0]], 32 * parts[i][1]
+        where = (slice(lo, hi), slice(r0, r0 + 32))
+        return pltpu.make_async_copy(grad_weight.at[where], grad_weight_hbm.at[where], leave.at[i])
+
+    through = [
+        pltpu.make_async_copy(out_in, out_feats, leave.at[4]),
+        pltpu.make_async_copy(feats_in, grad_feats, leave.at[5]),
+    ]
+    for i in range(4):
+        load(i).start()
+    for one in through:
+        one.start()
+    for i, (c, half) in enumerate(parts):
+        lo, hi = CHUNKS[c]
+        load(i).wait()
+        for xx in range(NX):
+            values = decode(codes[c, half, xx].reshape(16, 16, 128), hi - lo)
+            r0, l0 = half * 32 + (xx // 2) * 16, (xx % 2) * 128
+            values = jnp.swapaxes(values, 0, 1)
+            grad_weight[lo:hi, r0 : r0 + 16, l0 : l0 + 128] = values[: hi - lo]
+        store(i).start()
+    for i in range(4):
+        store(i).wait()
+    for one in through:
+        one.wait()
 
 
 def body(feats, weight, grad_out, neighbors, send_rows, send_counts):
-    vmem = pl.BlockSpec(memory_space=pltpu.VMEM)
+    hbm = pl.BlockSpec(memory_space=pltpu.HBM)
     out_feats, grad_feats, codes = pl.pallas_call(
         kernel,
         out_shape=(
@@ -446,9 +498,18 @@
             jax.ShapeDtypeStruct((SHARE, VOX), F32),
             jax.ShapeDtypeStruct((2, 2, NX, 256, 128), I16),
         ),
-        in_specs=[vmem] * 6,
-        out_specs=[vmem] * 3,
+        in_specs=[hbm] * 6,
+        out_specs=[hbm] * 3,
         scratch_shapes=[
+            pltpu.VMEM((SHARE, VOX), BF16),
+            pltpu.VMEM((KVOL, SHARE, C), BF16),
+            pltpu.VMEM((SHARE, VOX), BF16),
+            pltpu.VMEM((KVOL, VOX), jnp.int32),
+            pltpu.VMEM((1, HALO), jnp.int32),
+            pltpu.VMEM((8, DOM), jnp.int32),
+            pltpu.VMEM((SHARE, VOX), BF16),
+            pltpu.VMEM((SHARE, VOX), F32),
+            pltpu.VMEM((2, 2, NX, 256, 128), I16),
             pltpu.VMEM((VOX, 128), jnp.int32),
             pltpu.VMEM((KVOL, VOX, COLS), BF16),
             pltpu.VMEM((KVOL, VOX, C), BF16),
@@ -472,6 +533,7 @@
             pltpu.VMEM((8, 16, 128), F32),
             pltpu.SemaphoreType.DMA((105,)),
             pltpu.SemaphoreType.DMA((105,)),
+            pltpu.SemaphoreType.DMA((12,)),
         ],
         compiler_params=pltpu.CompilerParams(
             collective_id=0, has_side_effects=True, vmem_limit_bytes=56 * 1024 * 1024
@@ -484,8 +546,14 @@
             jax.ShapeDtypeStruct((SHARE, VOX), F32),
             jax.ShapeDtypeStruct((KVOL, SHARE, C), F32),
         ),
-        in_specs=[vmem] * 3,
-        out_specs=[vmem] * 3,
+        in_specs=[hbm] * 3,
+        out_specs=[hbm] * 3,
+        scratch_shapes=[
+            pltpu.VMEM((2, 2, NX, 256, 128), I16),
+            pltpu.VMEM((KVOL, SHARE, C), F32),
+            pltpu.SemaphoreType.DMA((4,)),
+            pltpu.SemaphoreType.DMA((6,)),
+        ],
         compiler_params=pltpu.CompilerParams(vmem_limit_bytes=60 * 1024 * 1024),
     )(codes, out_feats, grad_feats)
 

time: 77.7 us -> 77.4 us (level)
    pallas_call x1, Pallas kernels: 73.8 us -> 70.9 us  [body(): pl.pallas_call(kernel, out_shape=(jax.ShapeDtypeStruct((SHARE, VOX), BF16...]
    pallas_call x1, Pallas kernels: 3.12 us -> 5.66 us  [body(): pl.pallas_call(finish, out_shape=(jax.ShapeDtypeStruct((SHARE, VOX), BF16...]
where the time goes in v3:
time: 77.4 us; the launch traced here: 77.2 us
  Pallas kernels  76.6 us (99%)
    pallas_call x1, Pallas kernels, body(): pl.pallas_call(kernel, out_shape=(jax.ShapeDtypeStruct((SHARE, VOX), BF16...  70.9 us
    pallas_call x1, Pallas kernels, body(): pl.pallas_call(finish, out_shape=(jax.ShapeDtypeStruct((SHARE, VOX), BF16...  5.66 us

profile of v3, /device:TPU:1, one launch (start us, length us, event | category | flops | bytes accessed | tf_op | source)
XLA Modules:
  0.0 77.2 jit_solution(18251335308337146933)
XLA Ops:
  0.6 70.9 %shard_map.85 = (bf16[64,384]{1,0:T(8,128)(2,1)}, f32[64,384]{1,0:T(8,128)}, s16[2,2,4,256,128]{4,3,2,1,0:T(8,128)(2,1)}) custom-call(bf16[64,384]{1,0:T(8,128)(2,1)} %feats_hbm.1, bf16[27,64,256]{2,1,0:T(8,128)(2,1)} %weight_hbm.1, bf16[64,384]{1,0:T(8,128)(2,1)} %grad_out_hbm.1, s32[27,384]{1,0:T(8,128)} %neighbors_hbm.1, s32[1,256]{1,0:T(1,128)} %send_rows_hbm.1, ...), custom_call_target="tpu_custom_call" | custom-call | tf_op jit(solution)/shard_map/pallas_call | solution.py:494
  71.6 5.7 %shard_map.86 = (bf16[64,384]{1,0:T(8,128)(2,1)}, f32[64,384]{1,0:T(8,128)}, f32[27,64,256]{2,1,0:T(8,128)}) custom-call(s16[2,2,4,256,128]{4,3,2,1,0:T(8,128)(2,1)} %get-tuple-element.6.codes_hbm, bf16[64,384]{1,0:T(8,128)(2,1)} %get-tuple-element.7.out_in, f32[64,384]{1,0:T(8,128)} %get-tuple-element.8.feats_in), custom_call_target="tpu_custom_call" | custom-call | tf_op jit(solution)/shard_map/pallas_call | solution.py:542

commit v4 on v2

--- a/solution.py
+++ b/solution.py
@@ -56,11 +56,12 @@
 
 
 def kernel(
-    feats, weight, grad_out, neighbors, send_rows, send_counts,
-    out_feats, grad_feats, codes,
+    feats_hbm, weight_hbm, grad_out_hbm, neighbors_hbm, send_rows_hbm, send_counts_hbm,
+    out_feats_hbm, grad_feats_hbm, codes_hbm,
+    feats, weight, grad_out, neighbors, send_rows, send_counts, out_feats, grad_feats, codes,
     nbr_t, onehot, picked, spread_hi, spread_lo, share_all, halo_out, halo_in, halo_all,
     table, wg, pair_in, x_out, x_in, x_sum, z_out, z_in, tg, tg_in, back_out, back_in,
-    send, recv,
+    send, recv, local,
 ):
     me = lax.axis_index("dom")
     sub = lax.axis_index("sub")
@@ -82,6 +83,9 @@
     def z_peer(d):
         return lax.rem(z + d, NZ)
 
+    def far_first(i):
+        return NZ // 2 + ((i + 1) // 2) * (2 * lax.rem(i, 2) - 1)
+
     def y_peer(d):
         return lax.rem(sub + d, SUB)
 
@@ -106,15 +110,38 @@
     peers += [(wrap(me + hop), sub) for hop in HOPS]
     peers += [(twin, sub)]
     peers += [(at(x_peer(d), z, core), sub) for d in range(1, NX)]
+    def load(i):
+        pairs = (
+            (send_counts_hbm, send_counts), (send_rows_hbm, send_rows), (feats_hbm, feats),
+            (neighbors_hbm, neighbors), (grad_out_hbm, grad_out), (weight_hbm, weight),
+        )
+        return pltpu.make_async_copy(pairs[i][0], pairs[i][1], local.at[i])
+
+    def store(i):
+        pairs = [(out_feats, out_feats_hbm), (grad_feats, grad_feats_hbm)]
+        pairs += [(codes.at[c, half], codes_hbm.at[c, half]) for c in range(2) for half in (core, 1 - core)]
+        return pltpu.make_async_copy(pairs[i][0], pairs[i][1], local.at[6 + i])
+
+    with jax.named_scope("loads_first"):
+        for i in range(3):
+            load(i).start()
+
     with jax.named_scope("barrier_signals"):
+        @pl.loop(0, NZ - 1)
+        def _(i):
+            peer = (at(x, z_peer(far_first(i)), core), sub)
+            pl.semaphore_signal(barrier, inc=1, device_id=peer, device_id_type=MESH)
+
         for peer in peers:
             pl.semaphore_signal(barrier, inc=1, device_id=peer, device_id_type=MESH)
 
-        @pl.loop(1, NZ)
-        def _(d):
-            pl.semaphore_signal(barrier, inc=1, device_id=(at(x, z_peer(d), core), sub), device_id_type=MESH)
+    with jax.named_scope("loads"):
+        for i in range(3, 6):
+            load(i).start()
 
     with jax.named_scope("boundary_tiles"):
+        for i in range(3):
+            load(i).wait()
         lane = lax.broadcasted_iota(jnp.int32, (1, HALO), 1)
         mine = send_counts[...]
         mine = jnp.where(lax.broadcasted_iota(jnp.int32, (8, DOM), 1) == me, mine, 0).astype(F32)
@@ -147,6 +174,8 @@
         share_all[sub] = feats[...]
 
     with jax.named_scope("transpose_maps"):
+        for i in (3, 4, 5):
+            load(i).wait()
         nbr_t[...] = jnp.concatenate(
             [neighbors[...], jnp.zeros((128 - KVOL, VOX), jnp.int32)], axis=0
         ).T
@@ -255,7 +284,7 @@
         for xx in range(NX):
             both = wg[c, core, xx] + pair_in[c, xx]
             x_out[c, xx] = encode(both.reshape(16, 16, 128), hi - lo).reshape(256, 128)
-        for d in range(1, NX):
+        for d in (2, 1, 3):
             x_copy(c, d).start()
 
     def x_to_z(c):
@@ -268,9 +297,9 @@
         x_sum[c] = total.reshape(256, 128)
         z_out[c] = encode(total, hi - lo).reshape(256, 128)
 
-        @pl.loop(1, NZ)
-        def _(d):
-            z_copy(c, d).start()
+        @pl.loop(0, NZ - 1)
+        def _(i):
+            z_copy(c, far_first(i)).start()
 
     with jax.named_scope("wg_rows"):
         for c, (lo, hi) in enumerate(CHUNKS):
@@ -292,13 +321,8 @@
     with jax.named_scope("pair_b"):
         pair_copy(1).start()
 
-    with jax.named_scope("x_to_z_a"):
-        x_to_z(0)
-    with jax.named_scope("pair_to_x_b"):
-        pair_to_x(1)
-
-    with jax.named_scope("spread"):
-        @pl.loop(0, KVOL // UNROLL)
+    def spread(first, last):
+        @pl.loop(first, last)
         def _(g):
             for j in range(UNROLL):
                 k = g * UNROLL + j
@@ -306,6 +330,16 @@
                 high = total.astype(BF16)
                 spread_hi[k] = high
                 spread_lo[k] = (total - high.astype(F32)).astype(BF16)
+
+    with jax.named_scope("spread_a"):
+        spread(0, 5)
+    with jax.named_scope("pair_to_x_b"):
+        pair_to_x(1)
+    with jax.named_scope("spread_b"):
+        spread(5, 9)
+
+    with jax.named_scope("x_to_z_a"):
+        x_to_z(0)
 
     with jax.named_scope("table_grad"):
         total = None
@@ -338,25 +372,40 @@
         scaled = total * (1.0 / math.sqrt(VOX * DOM))
         codes[c, core, x, own_tile(z)] = encode(scaled, hi - lo)
 
-        @pl.loop(1, NZ)
-        def _(d):
-            gz_copy(c, d).start()
+        @pl.loop(0, NZ - 1)
+        def _(i):
+            gz_copy(c, far_first(i)).start()
 
     def z_to_x(c):
         @pl.loop(1, NZ)
         def _(d):
             gz_arrival(c, d).wait_recv()
 
-        for d in range(1, NX):
+        for d in (2, 1, 3):
             gx_copy(c, d).start()
 
     def x_to_pair(c):
         for d in range(1, NX):
             gx_arrival(c, d).wait_recv()
         gpair_copy(c).start()
+        store(2 + 2 * c).start()
 
     with jax.named_scope("z_reduce_a"):
         z_reduce(0)
+
+    with jax.named_scope("tg_sum"):
+        for d in range(1, SUB):
+            tg_copy(d).wait_recv()
+        mine_tg = tg[sub] + tg_in[0] + tg_in[1] + tg_in[2]
+        tail = mine_tg[:, VOX:].T
+        back_out[...] = jnp.concatenate([tail[:128], tail[128:]], axis=1).reshape(8, 16, 128)
+
+    def back_copy(n):
+        return copy("back", n, back_out.at[n], back_in.at[n], (wrap(me - HOPS[n]), sub))
+
+    with jax.named_scope("back_sends"):
+        for n in range(8):
+            back_copy(n).start()
 
     with jax.named_scope("out_feats"):
         def out_step(g, acc):
@@ -365,23 +414,10 @@
             return acc
 
         out_feats[...] = lax.fori_loop(0, KVOL // UNROLL, out_step, jnp.zeros((SHARE, VOX), F32)).astype(BF16)
+        store(0).start()
 
     with jax.named_scope("z_reduce_b"):
         z_reduce(1)
-
-    with jax.named_scope("tg_sum"):
-        for d in range(1, SUB):
-            tg_copy(d).wait_recv()
-        mine_tg = tg[sub] + tg_in[0] + tg_in[1] + tg_in[2]
-        tail = mine_tg[:, VOX:].T
-        back_out[...] = jnp.concatenate([tail[:128], tail[128:]], axis=1).reshape(8, 16, 128)
-
-    def back_copy(n):
-        return copy("back", n, back_out.at[n], back_in.at[n], (wrap(me - HOPS[n]), sub))
-
-    with jax.named_scope("back_sends"):
-        for n in range(8):
-            back_copy(n).start()
 
     with jax.named_scope("z_back"):
         z_to_x(0)
@@ -399,10 +435,12 @@
         back_hi = back.astype(BF16)
         back_lo = (back - back_hi.astype(F32)).astype(BF16)
         grad_feats[...] = mine_tg[:, :VOX] + dot(back_hi, pick, NT) + dot(back_lo, pick, NT)
+        store(1).start()
 
     with jax.named_scope("pair_back"):
-        gpair_arrival(0).wait_recv()
-        gpair_arrival(1).wait_recv()
+        for c in range(2):
+            gpair_arrival(c).wait_recv()
+            store(3 + 2 * c).start()
 
     with jax.named_scope("drain"):
         for d in range(1, SUB):
@@ -423,6 +461,9 @@
             def _(d):
                 z_copy(c, d).wait_send()
                 gz_copy(c, d).wait_send()
+    with jax.named_scope("stores"):
+        for i in range(6):
+            store(i).wait()
 
 
 def finish(codes, out_in, feats_in, out_feats, grad_feats, grad_weight):
@@ -438,6 +479,7 @@
 
 
 def body(feats, weight, grad_out, neighbors, send_rows, send_counts):
+    hbm = pl.BlockSpec(memory_space=pltpu.HBM)
     vmem = pl.BlockSpec(memory_space=pltpu.VMEM)
     out_feats, grad_feats, codes = pl.pallas_call(
         kernel,
@@ -446,9 +488,18 @@
             jax.ShapeDtypeStruct((SHARE, VOX), F32),
             jax.ShapeDtypeStruct((2, 2, NX, 256, 128), I16),
         ),
-        in_specs=[vmem] * 6,
-        out_specs=[vmem] * 3,
+        in_specs=[hbm] * 6,
+        out_specs=[hbm] * 3,
         scratch_shapes=[
+            pltpu.VMEM((SHARE, VOX), BF16),
+            pltpu.VMEM((KVOL, SHARE, C), BF16),
+            pltpu.VMEM((SHARE, VOX), BF16),
+            pltpu.VMEM((KVOL, VOX), jnp.int32),
+            pltpu.VMEM((1, HALO), jnp.int32),
+            pltpu.VMEM((8, DOM), jnp.int32),
+            pltpu.VMEM((SHARE, VOX), BF16),
+            pltpu.VMEM((SHARE, VOX), F32),
+            pltpu.VMEM((2, 2, NX, 256, 128), I16),
             pltpu.VMEM((VOX, 128), jnp.int32),
             pltpu.VMEM((KVOL, VOX, COLS), BF16),
             pltpu.VMEM((KVOL, VOX, C), BF16),
@@ -472,6 +523,7 @@
             pltpu.VMEM((8, 16, 128), F32),
             pltpu.SemaphoreType.DMA((105,)),
             pltpu.SemaphoreType.DMA((105,)),
+            pltpu.SemaphoreType.DMA((12,)),
         ],
         compiler_params=pltpu.CompilerParams(
             collective_id=0, has_side_effects=True, vmem_limit_bytes=56 * 1024 * 1024

time: 77.7 us -> 72.9 us (0.938)
  Pallas kernels: 76.9 us -> 72.1 us
    pallas_call x1, Pallas kernels: 73.8 us -> 68.9 us  [body(): pl.pallas_call(kernel, out_shape=(jax.ShapeDtypeStruct((SHARE, VOX), BF16...]
where the time goes in v4:
time: 72.9 us; the launch traced here: 72.7 us
  Pallas kernels  72.1 us (99%)
    pallas_call x1, Pallas kernels, body(): pl.pallas_call(kernel, out_shape=(jax.ShapeDtypeStruct((SHARE, VOX), BF16...  68.9 us
    pallas_call x1, Pallas kernels, body(): pl.pallas_call(finish, out_shape=(jax.ShapeDtypeStruct((SHARE, VOX), BF16...  3.12 us

profile of v4, /device:TPU:1, one launch (start us, length us, event | category | flops | bytes accessed | tf_op | source)
XLA Modules:
  0.0 72.7 jit_solution(6222370322611006156)
XLA Ops:
  0.6 68.9 %shard_map.85 = (bf16[64,384]{1,0:T(8,128)(2,1)}, f32[64,384]{1,0:T(8,128)}, s16[2,2,4,256,128]{4,3,2,1,0:T(8,128)(2,1)}) custom-call(bf16[64,384]{1,0:T(8,128)(2,1)} %feats_hbm.1, bf16[27,64,256]{2,1,0:T(8,128)(2,1)} %weight_hbm.1, bf16[64,384]{1,0:T(8,128)(2,1)} %grad_out_hbm.1, s32[27,384]{1,0:T(8,128)} %neighbors_hbm.1, s32[1,256]{1,0:T(1,128)} %send_rows_hbm.1, ...), custom_call_target="tpu_custom_call" | custom-call | tf_op jit(solution)/shard_map/pallas_call | solution.py:484
  69.6 3.1 %shard_map.86 = (bf16[64,384]{1,0:T(8,128)(2,1)}, f32[64,384]{1,0:T(8,128)}, f32[27,64,256]{2,1,0:T(8,128)}) custom-call(s16[2,2,4,256,128]{4,3,2,1,0:T(8,128)(2,1)} %get-tuple-element.6.codes, bf16[64,384]{1,0:T(8,128)(2,1)} %get-tuple-element.7.out_in, f32[64,384]{1,0:T(8,128)} %get-tuple-element.8.feats_in), custom_call_target="tpu_custom_call" | custom-call | tf_op jit(solution)/shard_map/pallas_call | solution.py:532

commit v5 on v4

--- a/solution.py
+++ b/solution.py
@@ -191,6 +191,19 @@
             for j in range(UNROLL):
                 onehot[g * UNROLL + j] = (now[:, j : j + 1] == slot).astype(F32).astype(BF16)
 
+    def spread(first, last):
+        @pl.loop(first, last)
+        def _(g):
+            for j in range(UNROLL):
+                k = g * UNROLL + j
+                total = dot(grad_out[...], onehot[k], NN)
+                high = total.astype(BF16)
+                spread_hi[k] = high
+                spread_lo[k] = (total - high.astype(F32)).astype(BF16)
+
+    with jax.named_scope("spread_a"):
+        spread(0, 5)
+
     def gather_own(first, last):
         @pl.loop(first // UNROLL, last // UNROLL)
         def _(g):
@@ -203,7 +216,7 @@
             share_copy(d).wait_recv()
         table[0:VOX] = share_all[...].reshape(C, VOX).T
     with jax.named_scope("gather_own_a"):
-        gather_own(0, 15)
+        gather_own(0, 9)
 
     with jax.named_scope("halo_arrival"):
         for n in range(8):
@@ -213,7 +226,7 @@
         halo_all[sub] = halo_in[...]
 
     with jax.named_scope("gather_own_b"):
-        gather_own(15, 27)
+        gather_own(9, 27)
 
     with jax.named_scope("table_halo"):
         for d in range(1, SUB):
@@ -229,7 +242,7 @@
         return copy("pair", c, wg.at[c, 1 - core], pair_in.at[c], (twin, sub))
 
     def x_copy(c, d):
-        return copy("x", 3 * c + d - 1, x_out.at[c, x_peer(d)], x_in.at[c, d - 1], (at(x_peer(d), z, core), sub))
+        return copy("x", 3 * c + d - 1, x_out.at[c, d - 1], x_in.at[c, d - 1], (at(x_peer(d), z, core), sub))
 
     def own_tile(zz):
         return pl.ds(pl.multiple_of(zz * 16, 16), 16)
@@ -281,10 +294,9 @@
     def pair_to_x(c):
         lo, hi = CHUNKS[c]
         pair_copy(c).wait_recv()
-        for xx in range(NX):
-            both = wg[c, core, xx] + pair_in[c, xx]
-            x_out[c, xx] = encode(both.reshape(16, 16, 128), hi - lo).reshape(256, 128)
         for d in (2, 1, 3):
+            both = wg[c, core, x_peer(d)] + pair_in[c, x_peer(d)]
+            x_out[c, d - 1] = encode(both.reshape(16, 16, 128), hi - lo).reshape(256, 128)
             x_copy(c, d).start()
 
     def x_to_z(c):
@@ -321,18 +333,6 @@
     with jax.named_scope("pair_b"):
         pair_copy(1).start()
 
-    def spread(first, last):
-        @pl.loop(first, last)
-        def _(g):
-            for j in range(UNROLL):
-                k = g * UNROLL + j
-                total = dot(grad_out[...], onehot[k], NN)
-                high = total.astype(BF16)
-                spread_hi[k] = high
-                spread_lo[k] = (total - high.astype(F32)).astype(BF16)
-
-    with jax.named_scope("spread_a"):
-        spread(0, 5)
     with jax.named_scope("pair_to_x_b"):
         pair_to_x(1)
     with jax.named_scope("spread_b"):
@@ -422,6 +422,24 @@
     with jax.named_scope("z_back"):
         z_to_x(0)
         z_to_x(1)
+    with jax.named_scope("drain_early"):
+        for d in range(1, SUB):
+            share_copy(d).wait_send()
+            fwd_copy(d).wait_send()
+            tg_copy(d).wait_send()
+        for n in range(8):
+            halo_copy(n).wait_send()
+            back_copy(n).wait_send()
+        for c in range(2):
+            pair_copy(c).wait_send()
+            for d in range(1, NX):
+                x_copy(c, d).wait_send()
+
+            @pl.loop(1, NZ)
+            def _(d):
+                z_copy(c, d).wait_send()
+                gz_copy(c, d).wait_send()
+
     with jax.named_scope("x_back"):
         x_to_pair(0)
         x_to_pair(1)
@@ -443,24 +461,10 @@
             store(3 + 2 * c).start()
 
     with jax.named_scope("drain"):
-        for d in range(1, SUB):
-            share_copy(d).wait_send()
-            fwd_copy(d).wait_send()
-            tg_copy(d).wait_send()
-        for n in range(8):
-            halo_copy(n).wait_send()
-            back_copy(n).wait_send()
         for c in range(2):
-            pair_copy(c).wait_send()
             gpair_copy(c).wait_send()
             for d in range(1, NX):
-                x_copy(c, d).wait_send()
                 gx_copy(c, d).wait_send()
-
-            @pl.loop(1, NZ)
-            def _(d):
-                z_copy(c, d).wait_send()
-                gz_copy(c, d).wait_send()
     with jax.named_scope("stores"):
         for i in range(6):
             store(i).wait()
@@ -512,7 +516,7 @@
             pltpu.VMEM((COLS, C), BF16),
             pltpu.VMEM((2, 2, NX, 256, 128), F32),
             pltpu.VMEM((2, NX, 256, 128), F32),
-            pltpu.VMEM((2, NX, 256, 128), I16),
+            pltpu.VMEM((2, NX - 1, 256, 128), I16),
             pltpu.VMEM((2, NX - 1, 256, 128), I16),
             pltpu.VMEM((2, 256, 128), F32),
             pltpu.VMEM((2, 256, 128), I16),

time: 72.9 us -> 72.1 us (0.989)
  Pallas kernels: 72.1 us -> 71.3 us
    pallas_call x1, Pallas kernels: 68.9 us -> 68.1 us  [body(): pl.pallas_call(kernel, out_shape=(jax.ShapeDtypeStruct((SHARE, VOX), BF16...]
where the time goes in v5:
time: 72.1 us; the launch traced here: 71.9 us
  Pallas kernels  71.3 us (99%)
    pallas_call x1, Pallas kernels, body(): pl.pallas_call(kernel, out_shape=(jax.ShapeDtypeStruct((SHARE, VOX), BF16...  68.1 us
    pallas_call x1, Pallas kernels, body(): pl.pallas_call(finish, out_shape=(jax.ShapeDtypeStruct((SHARE, VOX), BF16...  3.12 us

profile of v5, /device:TPU:1, one launch (start us, length us, event | category | flops | bytes accessed | tf_op | source)
XLA Modules:
  0.0 71.9 jit_solution(13613890008831484590)
XLA Ops:
  0.6 68.1 %shard_map.85 = (bf16[64,384]{1,0:T(8,128)(2,1)}, f32[64,384]{1,0:T(8,128)}, s16[2,2,4,256,128]{4,3,2,1,0:T(8,128)(2,1)}) custom-call(bf16[64,384]{1,0:T(8,128)(2,1)} %feats_hbm.1, bf16[27,64,256]{2,1,0:T(8,128)(2,1)} %weight_hbm.1, bf16[64,384]{1,0:T(8,128)(2,1)} %grad_out_hbm.1, s32[27,384]{1,0:T(8,128)} %neighbors_hbm.1, s32[1,256]{1,0:T(1,128)} %send_rows_hbm.1, ...), custom_call_target="tpu_custom_call" | custom-call | tf_op jit(solution)/shard_map/pallas_call | solution.py:488
  68.8 3.1 %shard_map.86 = (bf16[64,384]{1,0:T(8,128)(2,1)}, f32[64,384]{1,0:T(8,128)}, f32[27,64,256]{2,1,0:T(8,128)}) custom-call(s16[2,2,4,256,128]{4,3,2,1,0:T(8,128)(2,1)} %get-tuple-element.6.codes, bf16[64,384]{1,0:T(8,128)(2,1)} %get-tuple-element.7.out_in, f32[64,384]{1,0:T(8,128)} %get-tuple-element.8.feats_in), custom_call_target="tpu_custom_call" | custom-call | tf_op jit(solution)/shard_map/pallas_call | solution.py:536

commit v6 on v5

--- a/solution.py
+++ b/solution.py
@@ -57,8 +57,8 @@
 
 def kernel(
     feats_hbm, weight_hbm, grad_out_hbm, neighbors_hbm, send_rows_hbm, send_counts_hbm,
-    out_feats_hbm, grad_feats_hbm, codes_hbm,
-    feats, weight, grad_out, neighbors, send_rows, send_counts, out_feats, grad_feats, codes,
+    out_feats, grad_feats, codes,
+    feats, weight, grad_out, neighbors, send_rows, send_counts,
     nbr_t, onehot, picked, spread_hi, spread_lo, share_all, halo_out, halo_in, halo_all,
     table, wg, pair_in, x_out, x_in, x_sum, z_out, z_in, tg, tg_in, back_out, back_in,
     send, recv, local,
@@ -116,11 +116,6 @@
             (neighbors_hbm, neighbors), (grad_out_hbm, grad_out), (weight_hbm, weight),
         )
         return pltpu.make_async_copy(pairs[i][0], pairs[i][1], local.at[i])
-
-    def store(i):
-        pairs = [(out_feats, out_feats_hbm), (grad_feats, grad_feats_hbm)]
-        pairs += [(codes.at[c, half], codes_hbm.at[c, half]) for c in range(2) for half in (core, 1 - core)]
-        return pltpu.make_async_copy(pairs[i][0], pairs[i][1], local.at[6 + i])
 
     with jax.named_scope("loads_first"):
         for i in range(3):
@@ -388,7 +383,6 @@
         for d in range(1, NX):
             gx_arrival(c, d).wait_recv()
         gpair_copy(c).start()
-        store(2 + 2 * c).start()
 
     with jax.named_scope("z_reduce_a"):
         z_reduce(0)
@@ -414,7 +408,6 @@
             return acc
 
         out_feats[...] = lax.fori_loop(0, KVOL // UNROLL, out_step, jnp.zeros((SHARE, VOX), F32)).astype(BF16)
-        store(0).start()
 
     with jax.named_scope("z_reduce_b"):
         z_reduce(1)
@@ -453,21 +446,16 @@
         back_hi = back.astype(BF16)
         back_lo = (back - back_hi.astype(F32)).astype(BF16)
         grad_feats[...] = mine_tg[:, :VOX] + dot(back_hi, pick, NT) + dot(back_lo, pick, NT)
-        store(1).start()
 
     with jax.named_scope("pair_back"):
         for c in range(2):
             gpair_arrival(c).wait_recv()
-            store(3 + 2 * c).start()
 
     with jax.named_scope("drain"):
         for c in range(2):
             gpair_copy(c).wait_send()
             for d in range(1, NX):
                 gx_copy(c, d).wait_send()
-    with jax.named_scope("stores"):
-        for i in range(6):
-            store(i).wait()
 
 
 def finish(codes, out_in, feats_in, out_feats, grad_feats, grad_weight):
@@ -488,12 +476,12 @@
     out_feats, grad_feats, codes = pl.pallas_call(
         kernel,
         out_shape=(
-            jax.ShapeDtypeStruct((SHARE, VOX), BF16),
-            jax.ShapeDtypeStruct((SHARE, VOX), F32),
-            jax.ShapeDtypeStruct((2, 2, NX, 256, 128), I16),
+            pltpu.VMEM((SHARE, VOX), BF16),
+            pltpu.VMEM((SHARE, VOX), F32),
+            pltpu.VMEM((2, 2, NX, 256, 128), I16),
         ),
         in_specs=[hbm] * 6,
-        out_specs=[hbm] * 3,
+        out_specs=[vmem] * 3,
         scratch_shapes=[
             pltpu.VMEM((SHARE, VOX), BF16),
             pltpu.VMEM((KVOL, SHARE, C), BF16),
@@ -501,9 +489,6 @@
             pltpu.VMEM((KVOL, VOX), jnp.int32),
             pltpu.VMEM((1, HALO), jnp.int32),
             pltpu.VMEM((8, DOM), jnp.int32),
-            pltpu.VMEM((SHARE, VOX), BF16),
-            pltpu.VMEM((SHARE, VOX), F32),
-            pltpu.VMEM((2, 2, NX, 256, 128), I16),
             pltpu.VMEM((VOX, 128), jnp.int32),
             pltpu.VMEM((KVOL, VOX, COLS), BF16),
             pltpu.VMEM((KVOL, VOX, C), BF16),
@@ -527,7 +512,7 @@
             pltpu.VMEM((8, 16, 128), F32),
             pltpu.SemaphoreType.DMA((105,)),
             pltpu.SemaphoreType.DMA((105,)),
-            pltpu.SemaphoreType.DMA((12,)),
+            pltpu.SemaphoreType.DMA((6,)),
         ],
         compiler_params=pltpu.CompilerParams(
             collective_id=0, has_side_effects=True, vmem_limit_bytes=56 * 1024 * 1024
@@ -542,8 +527,8 @@
         ),
         in_specs=[vmem] * 3,
         out_specs=[vmem] * 3,
-        compiler_params=pltpu.CompilerParams(vmem_limit_bytes=60 * 1024 * 1024),
-    )(codes, out_feats, grad_feats)
+        compiler_params=pltpu.CompilerParams(vmem_limit_bytes=56 * 1024 * 1024),
+    )(*[pltpu.with_memory_space_constraint(one, pltpu.VMEM) for one in (codes, out_feats, grad_feats)])
 
 
 def solution(mesh):

time: 72.1 us -> 70.1 us (0.972)
  Pallas kernels: 71.3 us -> 69.3 us
    pallas_call x1, Pallas kernels: 3.12 us -> 1.87 us  [body(): pl.pallas_call(finish, out_shape=(jax.ShapeDtypeStruct((SHARE, VOX), BF16...]
    pallas_call x1, Pallas kernels: 68.1 us -> 67.4 us  [body(): pl.pallas_call(kernel, out_shape=(pltpu.VMEM((SHARE, VOX), BF16), pltpu.V...]
where the time goes in v6:
time: 70.1 us; the launch traced here: 69.9 us
  Pallas kernels  69.3 us (99%)
    pallas_call x1, Pallas kernels, body(): pl.pallas_call(kernel, out_shape=(pltpu.VMEM((SHARE, VOX), BF16), pltpu.V...  67.4 us
    pallas_call x1, Pallas kernels, body(): pl.pallas_call(finish, out_shape=(jax.ShapeDtypeStruct((SHARE, VOX), BF16...  1.87 us

profile of v6, /device:TPU:1, one launch (start us, length us, event | category | flops | bytes accessed | tf_op | source)
XLA Modules:
  0.0 69.9 jit_solution(6589720997293845996)
XLA Ops:
  0.6 67.4 %shard_map.85 = (bf16[64,384]{1,0:T(8,128)(2,1)S(1)}, f32[64,384]{1,0:T(8,128)S(1)}, s16[2,2,4,256,128]{4,3,2,1,0:T(8,128)(2,1)S(1)}) custom-call(bf16[64,384]{1,0:T(8,128)(2,1)} %feats_hbm.1, bf16[27,64,256]{2,1,0:T(8,128)(2,1)} %weight_hbm.1, bf16[64,384]{1,0:T(8,128)(2,1)} %grad_out_hbm.1, s32[27,384]{1,0:T(8,128)} %neighbors_hbm.1, ...), custom_call_target="tpu_custom_call" | custom-call | tf_op jit(solution)/shard_map/pallas_call | solution.py:476
  68.0 1.9 %shard_map.86 = (bf16[64,384]{1,0:T(8,128)(2,1)}, f32[64,384]{1,0:T(8,128)}, f32[27,64,256]{2,1,0:T(8,128)}) custom-call(s16[2,2,4,256,128]{4,3,2,1,0:T(8,128)(2,1)S(1)} %get-tuple-element.6.codes, bf16[64,384]{1,0:T(8,128)(2,1)S(1)} %get-tuple-element.7.out_in, f32[64,384]{1,0:T(8,128)S(1)} %get-tuple-element.8.feats_in), custom_call_target="tpu_custom_call" | custom-call | tf_op jit(solution)/shard_map/pallas_call | solution.py:521

commit v7 on v6

--- a/solution.py
+++ b/solution.py
@@ -61,7 +61,7 @@
     feats, weight, grad_out, neighbors, send_rows, send_counts,
     nbr_t, onehot, picked, spread_hi, spread_lo, share_all, halo_out, halo_in, halo_all,
     table, wg, pair_in, x_out, x_in, x_sum, z_out, z_in, tg, tg_in, back_out, back_in,
-    send, recv, local,
+    out_sum, send, recv, local,
 ):
     me = lax.axis_index("dom")
     sub = lax.axis_index("sub")
@@ -102,8 +102,8 @@
         slots[name] = 3 * base
     slots["halo"], slots["back"] = 9, 17
     slots["pair"], slots["gpair"] = 25, 27
-    slots["x"], slots["gx"] = 29, 35
-    slots["z"], slots["gz"] = 41, 73
+    slots["x"], slots["gx"] = 35, 41
+    slots["z"], slots["gz"] = 47, 79
 
     barrier = pltpu.get_barrier_semaphore()
     peers = [(me, y_peer(d)) for d in range(1, SUB)]
@@ -213,6 +213,13 @@
     with jax.named_scope("gather_own_a"):
         gather_own(0, 9)
 
+    with jax.named_scope("wg_rows"):
+        for c, (lo, hi) in enumerate(CHUNKS):
+            for row in range(hi - lo, 16):
+                for cc in range(2):
+                    for xx in range(NX):
+                        wg[c, cc, xx, pl.ds(row, 16, stride=16), :] = jnp.zeros((16, 128), F32)
+
     with jax.named_scope("halo_arrival"):
         for n in range(8):
             halo_copy(n).wait_recv()
@@ -261,13 +268,13 @@
         ref = codes.at[c, core, x_peer(NX - d)]
         return copy("gx", 3 * c + d - 1, ref, ref, (at(x_peer(d), z, core), sub))
 
-    def gpair_copy(c):
-        ref = codes.at[c, core]
-        return copy("gpair", c, ref, ref, (twin, sub))
-
-    def gpair_arrival(c):
-        ref = codes.at[c, 1 - core]
-        return copy("gpair", c, ref, ref, (twin, sub))
+    def gpair_copy(c, d):
+        ref = codes.at[c, core, x_peer(NX - d)]
+        return copy("gpair", NX * c + d, ref, ref, (twin, sub))
+
+    def gpair_arrival(c, d):
+        ref = codes.at[c, 1 - core, x_peer(NX - d)]
+        return copy("gpair", NX * c + d, ref, ref, (twin, sub))
 
     def gather(c, first, last):
         lo = CHUNKS[c][0]
@@ -308,13 +315,6 @@
         def _(i):
             z_copy(c, far_first(i)).start()
 
-    with jax.named_scope("wg_rows"):
-        for c, (lo, hi) in enumerate(CHUNKS):
-            for row in range(hi - lo, 16):
-                for cc in range(2):
-                    for xx in range(NX):
-                        wg[c, cc, xx, pl.ds(row, 16, stride=16), :] = jnp.zeros((16, 128), F32)
-
     with jax.named_scope("gather_a"):
         gather(0, 0, 15)
     with jax.named_scope("pair_a"):
@@ -378,12 +378,20 @@
 
         for d in (2, 1, 3):
             gx_copy(c, d).start()
+        gpair_copy(c, 0).start()
 
     def x_to_pair(c):
-        for d in range(1, NX):
+        for d in (1, 3, 2):
             gx_arrival(c, d).wait_recv()
-        gpair_copy(c).start()
-
+            gpair_copy(c, d).start()
+
+    def out_step(g, acc):
+        for j in range(UNROLL):
+            acc = acc + dot(weight[g * UNROLL + j], picked[g * UNROLL + j], NT)
+        return acc
+
+    with jax.named_scope("out_feats_a"):
+        out_sum[...] = lax.fori_loop(0, 5, out_step, jnp.zeros((SHARE, VOX), F32))
     with jax.named_scope("z_reduce_a"):
         z_reduce(0)
 
@@ -401,16 +409,11 @@
         for n in range(8):
             back_copy(n).start()
 
-    with jax.named_scope("out_feats"):
-        def out_step(g, acc):
-            for j in range(UNROLL):
-                acc = acc + dot(weight[g * UNROLL + j], picked[g * UNROLL + j], NT)
-            return acc
-
-        out_feats[...] = lax.fori_loop(0, KVOL // UNROLL, out_step, jnp.zeros((SHARE, VOX), F32)).astype(BF16)
-
     with jax.named_scope("z_reduce_b"):
         z_reduce(1)
+
+    with jax.named_scope("out_feats_b"):
+        out_feats[...] = lax.fori_loop(5, 9, out_step, out_sum[...]).astype(BF16)
 
     with jax.named_scope("z_back"):
         z_to_x(0)
@@ -449,11 +452,13 @@
 
     with jax.named_scope("pair_back"):
         for c in range(2):
-            gpair_arrival(c).wait_recv()
+            for d in range(NX):
+                gpair_arrival(c, d).wait_recv()
 
     with jax.named_scope("drain"):
         for c in range(2):
-            gpair_copy(c).wait_send()
+            for d in range(NX):
+                gpair_copy(c, d).wait_send()
             for d in range(1, NX):
                 gx_copy(c, d).wait_send()
 
@@ -510,8 +515,9 @@
             pltpu.VMEM((SUB - 1, SHARE, COLS), F32),
             pltpu.VMEM((8, 16, 128), F32),
             pltpu.VMEM((8, 16, 128), F32),
-            pltpu.SemaphoreType.DMA((105,)),
-            pltpu.SemaphoreType.DMA((105,)),
+            pltpu.VMEM((SHARE, VOX), F32),
+            pltpu.SemaphoreType.DMA((111,)),
+            pltpu.SemaphoreType.DMA((111,)),
             pltpu.SemaphoreType.DMA((6,)),
         ],
         compiler_params=pltpu.CompilerParams(

time: 70.1 us -> 69.5 us (level)
  no operation moved by 1% of the time
where the time goes in v7:
time: 69.5 us; the launch traced here: 69.4 us
  Pallas kernels  68.7 us (99%)
    pallas_call x1, Pallas kernels, body(): pl.pallas_call(kernel, out_shape=(pltpu.VMEM((SHARE, VOX), BF16), pltpu.V...  66.9 us
    pallas_call x1, Pallas kernels, body(): pl.pallas_call(finish, out_shape=(jax.ShapeDtypeStruct((SHARE, VOX), BF16...  1.87 us

profile of v7, /device:TPU:1, one launch (start us, length us, event | category | flops | bytes accessed | tf_op | source)
XLA Modules:
  0.0 69.4 jit_solution(9411724048102112269)
XLA Ops:
  0.6 66.9 %shard_map.85 = (bf16[64,384]{1,0:T(8,128)(2,1)S(1)}, f32[64,384]{1,0:T(8,128)S(1)}, s16[2,2,4,256,128]{4,3,2,1,0:T(8,128)(2,1)S(1)}) custom-call(bf16[64,384]{1,0:T(8,128)(2,1)} %feats_hbm.1, bf16[27,64,256]{2,1,0:T(8,128)(2,1)} %weight_hbm.1, bf16[64,384]{1,0:T(8,128)(2,1)} %grad_out_hbm.1, s32[27,384]{1,0:T(8,128)} %neighbors_hbm.1, ...), custom_call_target="tpu_custom_call" | custom-call | tf_op jit(solution)/shard_map/pallas_call | solution.py:481
  67.5 1.9 %shard_map.86 = (bf16[64,384]{1,0:T(8,128)(2,1)}, f32[64,384]{1,0:T(8,128)}, f32[27,64,256]{2,1,0:T(8,128)}) custom-call(s16[2,2,4,256,128]{4,3,2,1,0:T(8,128)(2,1)S(1)} %get-tuple-element.6.codes, bf16[64,384]{1,0:T(8,128)(2,1)S(1)} %get-tuple-element.7.out_in, f32[64,384]{1,0:T(8,128)S(1)} %get-tuple-element.8.feats_in), custom_call_target="tpu_custom_call" | custom-call | tf_op jit(solution)/shard_map/pallas_call | solution.py:527

commit v8 on v7

--- a/solution.py
+++ b/solution.py
@@ -303,10 +303,9 @@
 
     def x_to_z(c):
         lo, hi = CHUNKS[c]
-        for d in range(1, NX):
+        total = (wg[c, core, x] + pair_in[c, x]).reshape(16, 16, 128)
+        for d in (1, 3, 2):
             x_copy(c, d).wait_recv()
-        total = (wg[c, core, x] + pair_in[c, x]).reshape(16, 16, 128)
-        for d in range(1, NX):
             total = total + decode(x_in[c, d - 1].reshape(16, 16, 128), hi - lo)
         x_sum[c] = total.reshape(256, 128)
         z_out[c] = encode(total, hi - lo).reshape(256, 128)
@@ -359,11 +358,13 @@
     def z_reduce(c):
         lo, hi = CHUNKS[c]
 
-        @pl.loop(1, NZ)
-        def _(d):
-            z_copy(c, d).wait_recv()
-
-        total = x_sum[c, own_tile(z)] + jnp.sum(decode(z_in[c], hi - lo), axis=0)
+        total = x_sum[c, own_tile(z)]
+        for first, last in ((1, 5), (12, 16), (5, 12)):
+            @pl.loop(first, last)
+            def _(d):
+                z_copy(c, d).wait_recv()
+
+            total = total + jnp.sum(decode(z_in[c, first - 1 : last - 1], hi - lo), axis=0)
         scaled = total * (1.0 / math.sqrt(VOX * DOM))
         codes[c, core, x, own_tile(z)] = encode(scaled, hi - lo)
 

time: 69.5 us -> 69.6 us (level)
  no operation moved by 1% of the time
where the time goes in v8:
time: 69.6 us; the launch traced here: 69.5 us
  Pallas kernels  68.8 us (99%)
    pallas_call x1, Pallas kernels, body(): pl.pallas_call(kernel, out_shape=(pltpu.VMEM((SHARE, VOX), BF16), pltpu.V...  67 us
    pallas_call x1, Pallas kernels, body(): pl.pallas_call(finish, out_shape=(jax.ShapeDtypeStruct((SHARE, VOX), BF16...  1.87 us

profile of v8, /device:TPU:1, one launch (start us, length us, event | category | flops | bytes accessed | tf_op | source)
XLA Modules:
  0.0 69.5 jit_solution(9554930345288762158)
XLA Ops:
  0.6 67.0 %shard_map.85 = (bf16[64,384]{1,0:T(8,128)(2,1)S(1)}, f32[64,384]{1,0:T(8,128)S(1)}, s16[2,2,4,256,128]{4,3,2,1,0:T(8,128)(2,1)S(1)}) custom-call(bf16[64,384]{1,0:T(8,128)(2,1)} %feats_hbm.1, bf16[27,64,256]{2,1,0:T(8,128)(2,1)} %weight_hbm.1, bf16[64,384]{1,0:T(8,128)(2,1)} %grad_out_hbm.1, s32[27,384]{1,0:T(8,128)} %neighbors_hbm.1, ...), custom_call_target="tpu_custom_call" | custom-call | tf_op jit(solution)/shard_map/pallas_call | solution.py:482
  67.6 1.9 %shard_map.86 = (bf16[64,384]{1,0:T(8,128)(2,1)}, f32[64,384]{1,0:T(8,128)}, f32[27,64,256]{2,1,0:T(8,128)}) custom-call(s16[2,2,4,256,128]{4,3,2,1,0:T(8,128)(2,1)S(1)} %get-tuple-element.6.codes, bf16[64,384]{1,0:T(8,128)(2,1)S(1)} %get-tuple-element.7.out_in, f32[64,384]{1,0:T(8,128)S(1)} %get-tuple-element.8.feats_in), custom_call_target="tpu_custom_call" | custom-call | tf_op jit(solution)/shard_map/pallas_call | solution.py:528
